TPU v7x, 32 devices: a whole 2x2x4 slice. The times are simulated.
32 devices in a mesh: dp: 8 (over z, y), mp: 4 (over x, core).
Axes of the slice: x: 2, y: 2, z: 4, core: 2. Of those that a mesh axis runs over, the one named last changes fastest.
Arguments:
- activations: bfloat16 [32, 256, 1024], P('dp'), may hold values from -6 to 6
- segments: int32 [32, 256], P('dp'), may hold values from 0 to 2, as said below
- first_gain: float32 [2, 1024], replicated, may hold values from 0.5 to 1.5
- first_shift: float32 [2, 1024], replicated, may hold values from -1.5 to 1.5
- query_weight: bfloat16 [2, 1024, 1024], P(None, None, 'mp'), may hold values from -0.1875 to 0.1875
- key_weight: bfloat16 [2, 1024, 1024], P(None, None, 'mp'), may hold values from -0.1875 to 0.1875
- value_weight: bfloat16 [2, 1024, 1024], P(None, None, 'mp'), may hold values from -0.1875 to 0.1875
- query_bias: float32 [2, 1024], P(None, 'mp'), may hold values from -3 to 3
- value_bias: float32 [2, 1024], P(None, 'mp'), may hold values from -3 to 3
- out_weight: bfloat16 [2, 1024, 1024], P(None, None, 'mp'), may hold values from -0.75 to 0.75
- out_bias: float32 [2, 1024], replicated, may hold values from -1.5 to 1.5
- attend_scale: float32 [2, 1024], replicated, may hold values from 0.25 to 1.75
- second_gain: float32 [2, 1024], replicated, may hold values from 0.5 to 1.5
- second_shift: float32 [2, 1024], replicated, may hold values from -1.5 to 1.5
- up_weight: bfloat16 [2, 1024, 4096], P(None, None, 'mp'), may hold values from -0.1875 to 0.1875
- up_bias: float32 [2, 4096], P(None, 'mp'), may hold values from -1.5 to 1.5
- down_weight: bfloat16 [2, 1024, 4096], P(None, None, 'mp'), may hold values from -0.1875 to 0.1875
- down_bias: float32 [2, 1024], replicated, may hold values from -1.5 to 1.5
- feed_scale: float32 [2, 1024], replicated, may hold values from 0.25 to 1.75
- cotangent: bfloat16 [32, 256, 1024], P('dp'), may hold values from -6 to 6
Outputs:
- result: bfloat16 [32, 256, 1024], P('dp')
- input_grad: float32 [32, 256, 1024], P('dp')
- first_gain_grad: float32 [2, 1024], P(None, 'dp')
- first_shift_grad: float32 [2, 1024], P(None, 'dp')
- query_weight_grad: float32 [2, 1024, 1024], P(None, 'dp', 'mp')
- key_weight_grad: float32 [2, 1024, 1024], P(None, 'dp', 'mp')
- value_weight_grad: float32 [2, 1024, 1024], P(None, 'dp', 'mp')
- query_bias_grad: float32 [2, 1024], P(None, ('mp', 'dp'))
- value_bias_grad: float32 [2, 1024], P(None, ('mp', 'dp'))
- out_weight_grad: float32 [2, 1024, 1024], P(None, 'dp', 'mp')
- out_bias_grad: float32 [2, 1024], P(None, 'dp')
- attend_scale_grad: float32 [2, 1024], P(None, 'dp')
- second_gain_grad: float32 [2, 1024], P(None, 'dp')
- second_shift_grad: float32 [2, 1024], P(None, 'dp')
- up_weight_grad: float32 [2, 1024, 4096], P(None, 'dp', 'mp')
- up_bias_grad: float32 [2, 4096], P(None, ('mp', 'dp'))
- down_weight_grad: float32 [2, 1024, 4096], P(None, 'dp', 'mp')
- down_bias_grad: float32 [2, 1024], P(None, 'dp')
- feed_scale_grad: float32 [2, 1024], P(None, 'dp')
Inputs may be any that keep to these rules, and one draw needn't show every extreme that they name: `segments`: in every row the 197 slots of segment 0 form one run, the 50 slots of segment 1 form another, and every other slot holds 2.
All inputs are finite; a program needn't handle non-finite values.
Results may differ from a plain program's by a relative error of at most 0.025.
Values may be sent and summed in bfloat16 or wider, within the bound.
No kernel may reach another device: no remote copies, remote signals or barrier semaphores. Data moves between devices by JAX's collectives and lax.ppermute only.
A program may use at most 192 MiB of HBM per device.

v0:
```python
from functools import partial

import jax
import jax.numpy as jnp
from jax import lax
from jax.sharding import PartitionSpec as P

HD = 64


EPSILON = 1e-06
CONTRACT_ROWS = (((0,), (0,)), ((), ()))
CONTRACT_LAST = (((1,), (1,)), ((), ()))


def norm_rows(values, gain, shift):
    center = values - jnp.mean(values, axis=-1, keepdims=True)
    spread = jnp.mean(center * center, axis=-1, keepdims=True)
    return center * lax.rsqrt(spread + EPSILON) * gain + shift


def attention_pieces(current, weights_now, same_crop, rows, slots):
    normed = norm_rows(current, weights_now[0], weights_now[1]).astype(jnp.bfloat16)
    query = (
        jnp.dot(normed, weights_now[2], preferred_element_type=jnp.float32) + weights_now[5]
    ).astype(jnp.bfloat16)
    key_part = jnp.dot(normed, weights_now[3], preferred_element_type=jnp.float32).astype(
        jnp.bfloat16
    )
    value_part = (
        jnp.dot(normed, weights_now[4], preferred_element_type=jnp.float32) + weights_now[6]
    ).astype(jnp.bfloat16)
    heads_local = query.shape[1] // HD
    shape_heads = (rows, slots, heads_local, HD)
    query_heads = query.reshape(shape_heads)
    key_heads = key_part.reshape(shape_heads)
    value_heads = value_part.reshape(shape_heads)
    scores = jnp.einsum(
        "rqhd,rkhd->rhqk", query_heads, key_heads, preferred_element_type=jnp.float32
    ) * HD ** (-0.5)
    scores = jnp.where(same_crop, scores, -1e30)
    probs = jax.nn.softmax(scores, axis=-1)
    probs_low = probs.astype(jnp.bfloat16)
    mixed = jnp.einsum(
        "rhqk,rkhd->rqhd", probs_low, value_heads, preferred_element_type=jnp.float32
    )
    mixed = mixed.reshape(rows * slots, heads_local * HD).astype(jnp.bfloat16)
    return (normed, query_heads, key_heads, value_heads, probs, probs_low, mixed)


def feed_pieces(middle, weights_now):
    normed2 = norm_rows(middle, weights_now[10], weights_now[11]).astype(jnp.bfloat16)
    before_gelu = (
        jnp.dot(normed2, weights_now[12], preferred_element_type=jnp.float32) + weights_now[13]
    )
    activated = jax.nn.gelu(before_gelu, approximate=False).astype(jnp.bfloat16)
    return (normed2, before_gelu, activated)


def forward_layer(current, weights_now, same_crop, rows, slots):
    pieces = attention_pieces(current, weights_now, same_crop, rows, slots)
    partial_out = lax.dot_general(
        pieces[6], weights_now[7], CONTRACT_LAST, preferred_element_type=jnp.float32
    )
    attended = lax.psum(partial_out.astype(jnp.bfloat16), "mp").astype(jnp.float32)
    middle = current + weights_now[9] * (attended + weights_now[8])
    normed2, before_gelu, activated = feed_pieces(middle, weights_now)
    partial_feed = lax.dot_general(
        activated, weights_now[14], CONTRACT_LAST, preferred_element_type=jnp.float32
    )
    fed = lax.psum(partial_feed.astype(jnp.bfloat16), "mp").astype(jnp.float32)
    return (middle + weights_now[16] * (fed + weights_now[15]), attended, fed)


def backward_layer(grad, current, attended, fed, weights_now, same_crop, rows, slots):
    middle = current + weights_now[9] * (attended + weights_now[8])
    normed2, before_gelu, activated = feed_pieces(middle, weights_now)
    scaled_feed = weights_now[16] * grad
    grad_fed = scaled_feed.astype(jnp.bfloat16)
    down_bias_grad = jnp.sum(scaled_feed, axis=0)
    feed_scale_grad = jnp.sum(grad * (fed + weights_now[15]), axis=0)
    down_weight_grad = lax.dot_general(
        grad_fed, activated, CONTRACT_ROWS, preferred_element_type=jnp.float32
    )
    grad_activated = jnp.dot(grad_fed, weights_now[14], preferred_element_type=jnp.float32)
    gelu_value, gelu_pull = jax.vjp(partial(jax.nn.gelu, approximate=False), before_gelu)
    grad_before = gelu_pull(grad_activated)[0].astype(jnp.bfloat16)
    up_bias_grad = jnp.sum(grad_before, axis=0, dtype=jnp.float32)
    up_weight_grad = lax.dot_general(
        normed2, grad_before, CONTRACT_ROWS, preferred_element_type=jnp.float32
    )
    partial_normed2 = lax.dot_general(
        grad_before, weights_now[12], CONTRACT_LAST, preferred_element_type=jnp.float32
    )
    grad_normed2 = lax.psum(partial_normed2.astype(jnp.bfloat16), "mp").astype(jnp.float32)
    norm_value, second_pull = jax.vjp(norm_rows, middle, weights_now[10], weights_now[11])
    middle_part, second_gain_grad, second_shift_grad = second_pull(grad_normed2)
    grad_middle = grad + middle_part
    normed, query_heads, key_heads, value_heads, probs, probs_low, mixed = attention_pieces(
        current, weights_now, same_crop, rows, slots
    )
    scaled_attend = weights_now[9] * grad_middle
    grad_attended = scaled_attend.astype(jnp.bfloat16)
    out_bias_grad = jnp.sum(scaled_attend, axis=0)
    attend_scale_grad = jnp.sum(grad_middle * (attended + weights_now[8]), axis=0)
    out_weight_grad = lax.dot_general(
        grad_attended, mixed, CONTRACT_ROWS, preferred_element_type=jnp.float32
    )
    grad_mixed = jnp.dot(grad_attended, weights_now[7], preferred_element_type=jnp.float32).astype(
        jnp.bfloat16
    )
    grad_mixed = grad_mixed.reshape(query_heads.shape)
    grad_probs = jnp.einsum(
        "rqhd,rkhd->rhqk", grad_mixed, value_heads, preferred_element_type=jnp.float32
    )
    grad_value = jnp.einsum(
        "rhqk,rqhd->rkhd", probs_low, grad_mixed, preferred_element_type=jnp.float32
    ).astype(jnp.bfloat16)
    grad_scores = probs * (grad_probs - jnp.sum(probs * grad_probs, axis=-1, keepdims=True))
    grad_scores = grad_scores.astype(jnp.bfloat16)
    scale = HD ** (-0.5)
    grad_query = (
        jnp.einsum("rhqk,rkhd->rqhd", grad_scores, key_heads, preferred_element_type=jnp.float32)
        * scale
    ).astype(jnp.bfloat16)
    grad_key = (
        jnp.einsum("rhqk,rqhd->rkhd", grad_scores, query_heads, preferred_element_type=jnp.float32)
        * scale
    ).astype(jnp.bfloat16)
    tokens_local = rows * slots
    grad_query = grad_query.reshape(tokens_local, -1)
    grad_key = grad_key.reshape(tokens_local, -1)
    grad_value = grad_value.reshape(tokens_local, -1)
    query_weight_grad = lax.dot_general(
        normed, grad_query, CONTRACT_ROWS, preferred_element_type=jnp.float32
    )
    key_weight_grad = lax.dot_general(
        normed, grad_key, CONTRACT_ROWS, preferred_element_type=jnp.float32
    )
    value_weight_grad = lax.dot_general(
        normed, grad_value, CONTRACT_ROWS, preferred_element_type=jnp.float32
    )
    query_bias_grad = jnp.sum(grad_query, axis=0, dtype=jnp.float32)
    value_bias_grad = jnp.sum(grad_value, axis=0, dtype=jnp.float32)
    partial_normed = lax.dot_general(
        grad_query, weights_now[2], CONTRACT_LAST, preferred_element_type=jnp.float32
    )
    partial_normed = partial_normed + lax.dot_general(
        grad_key, weights_now[3], CONTRACT_LAST, preferred_element_type=jnp.float32
    )
    partial_normed = partial_normed + lax.dot_general(
        grad_value, weights_now[4], CONTRACT_LAST, preferred_element_type=jnp.float32
    )
    grad_normed = lax.psum(partial_normed.astype(jnp.bfloat16), "mp").astype(jnp.float32)
    first_value, first_pull = jax.vjp(norm_rows, current, weights_now[0], weights_now[1])
    current_part, first_gain_grad, first_shift_grad = first_pull(grad_normed)
    grad_current = grad_middle + current_part
    layer_grads = (
        first_gain_grad,
        first_shift_grad,
        query_weight_grad,
        key_weight_grad,
        value_weight_grad,
        query_bias_grad,
        value_bias_grad,
        out_weight_grad,
        out_bias_grad,
        attend_scale_grad,
        second_gain_grad,
        second_shift_grad,
        up_weight_grad,
        up_bias_grad,
        down_weight_grad,
        down_bias_grad,
        feed_scale_grad,
    )
    return (grad_current, layer_grads)


def per_device(
    activations,
    segments,
    first_gain,
    first_shift,
    query_weight,
    key_weight,
    value_weight,
    query_bias,
    value_bias,
    out_weight,
    out_bias,
    attend_scale,
    second_gain,
    second_shift,
    up_weight,
    up_bias,
    down_weight,
    down_bias,
    feed_scale,
    cotangent,
):
    rows, slots, width = activations.shape
    same_crop = (segments[:, :, None] == segments[:, None, :])[:, None]
    params = (
        first_gain,
        first_shift,
        query_weight,
        key_weight,
        value_weight,
        query_bias,
        value_bias,
        out_weight,
        out_bias,
        attend_scale,
        second_gain,
        second_shift,
        up_weight,
        up_bias,
        down_weight,
        down_bias,
        feed_scale,
    )
    layers = first_gain.shape[0]
    current = activations.astype(jnp.float32).reshape(rows * slots, width)
    kept = []
    for layer in range(layers):
        weights_now = tuple((p[layer] for p in params))
        following, attended, fed = forward_layer(current, weights_now, same_crop, rows, slots)
        kept.append((current, attended, fed))
        current = following
    result = current.reshape(rows, slots, width).astype(jnp.bfloat16)
    grad = cotangent.astype(jnp.float32).reshape(rows * slots, width)
    collected = [None] * layers
    for layer in reversed(range(layers)):
        weights_now = tuple((p[layer] for p in params))
        layer_input, attended, fed = kept[layer]
        grad, lg = backward_layer(
            grad, layer_input, attended, fed, weights_now, same_crop, rows, slots
        )
        collected[layer] = lg
    stacked = tuple((jnp.stack([entry[index] for entry in collected]) for index in range(17)))
    stacked = (
        lax.psum_scatter(stacked[0], "dp", scatter_dimension=1, tiled=True),
        lax.psum_scatter(stacked[1], "dp", scatter_dimension=1, tiled=True),
        lax.psum_scatter(stacked[2], "dp", scatter_dimension=1, tiled=True),
        lax.psum_scatter(stacked[3], "dp", scatter_dimension=1, tiled=True),
        lax.psum_scatter(stacked[4], "dp", scatter_dimension=1, tiled=True),
        lax.psum_scatter(stacked[5], "dp", scatter_dimension=1, tiled=True),
        lax.psum_scatter(stacked[6], "dp", scatter_dimension=1, tiled=True),
        lax.psum_scatter(stacked[7], "dp", scatter_dimension=1, tiled=True),
        lax.psum_scatter(stacked[8], "dp", scatter_dimension=1, tiled=True),
        lax.psum_scatter(stacked[9], "dp", scatter_dimension=1, tiled=True),
        lax.psum_scatter(stacked[10], "dp", scatter_dimension=1, tiled=True),
        lax.psum_scatter(stacked[11], "dp", scatter_dimension=1, tiled=True),
        lax.psum_scatter(stacked[12], "dp", scatter_dimension=1, tiled=True),
        lax.psum_scatter(stacked[13], "dp", scatter_dimension=1, tiled=True),
        lax.psum_scatter(stacked[14], "dp", scatter_dimension=1, tiled=True),
        lax.psum_scatter(stacked[15], "dp", scatter_dimension=1, tiled=True),
        lax.psum_scatter(stacked[16], "dp", scatter_dimension=1, tiled=True),
    )
    input_grad = grad.reshape(rows, slots, width)
    return (result, input_grad) + tuple(stacked)


def solution(mesh):
    return jax.shard_map(
        per_device,
        mesh=mesh,
        in_specs=(
            P("dp", None, None),
            P("dp", None),
            P(),
            P(),
            P(None, None, "mp"),
            P(None, None, "mp"),
            P(None, None, "mp"),
            P(None, "mp"),
            P(None, "mp"),
            P(None, None, "mp"),
            P(),
            P(),
            P(),
            P(),
            P(None, None, "mp"),
            P(None, "mp"),
            P(None, None, "mp"),
            P(),
            P(),
            P("dp", None, None),
        ),
        out_specs=(
            P("dp", None, None),
            P("dp", None, None),
            P(None, "dp"),
            P(None, "dp"),
            P(None, "dp", "mp"),
            P(None, "dp", "mp"),
            P(None, "dp", "mp"),
            P(None, ("mp", "dp")),
            P(None, ("mp", "dp")),
            P(None, "dp", "mp"),
            P(None, "dp"),
            P(None, "dp"),
            P(None, "dp"),
            P(None, "dp"),
            P(None, "dp", "mp"),
            P(None, ("mp", "dp")),
            P(None, "dp", "mp"),
            P(None, "dp"),
            P(None, "dp"),
        ),
        check_vma=False,
    )
```

profile of v0, /device:TPU:0, one launch (start us, length us, event | category | flops | bytes accessed | tf_op | source)
XLA Modules:
  0.0 1916.8 jit_solution(12943200775844317483)
XLA Ops:
  20.7 3.2 convolution_convert_fusion.9
  27.4 3.2 fusion.91
  33.9 4.8 fusion.180
  38.7 2.8 fusion.103
  45.4 53.8 %all-reduce.9.cloned.1.call-done = bf16[1024,1024]{1,0:T(8,128)(2,1)} async-done(((bf16[1024,1024]{1,0:T(8,128)(2,1)}), bf16[1024,1024]{1,0:T(8,128)(2,1)}) %all-reduce.9.cloned.1.call-update) | async-done | bytes 2097168 | tf_op jit(solution)/shard_map/psum | solution.py:65
  99.2 2.6 fusion.161
  105.3 12.4 multiply_convert_fusion.3
  119.0 3.7 fusion.74
  123.8 50.5 %all-reduce.11.cloned.1.call-done = bf16[1024,1024]{1,0:T(8,128)(2,1)} async-done(((bf16[1024,1024]{1,0:T(8,128)(2,1)}), bf16[1024,1024]{1,0:T(8,128)(2,1)}) %all-reduce.11.cloned.1.call-update) | async-done | bytes 2097168 | tf_op jit(solution)/shard_map/psum | solution.py:71
  174.3 3.7 fusion.167
  190.6 3.2 fusion.93
  197.1 4.7 fusion.181
  201.8 2.9 fusion.104
  208.4 4.3 fusion.20
  212.6 47.1 %all-reduce.13.cloned.1.call-done = bf16[1024,1024]{1,0:T(8,128)(2,1)} async-done(((bf16[1024,1024]{1,0:T(8,128)(2,1)}), bf16[1024,1024]{1,0:T(8,128)(2,1)}) %all-reduce.13.cloned.1.call-update) | async-done | bytes 2097168 | tf_op jit(solution)/shard_map/psum | solution.py:65
  259.8 3.6 fusion.166
  264.0 3.1 copy-done.96
  267.1 12.7 multiply_convert_fusion.2
  279.8 4.0 convert_reduce_fusion.5
  285.2 3.7 fusion.77
  289.0 51.6 %all-reduce.15.cloned.1.call-done = bf16[1024,1024]{1,0:T(8,128)(2,1)} async-done(((bf16[1024,1024]{1,0:T(8,128)(2,1)}), bf16[1024,1024]{1,0:T(8,128)(2,1)}) %all-reduce.15.cloned.1.call-update) | async-done | bytes 2097168 | tf_op jit(solution)/shard_map/psum | solution.py:95
  340.5 4.2 convert_reduce_fusion.3
  347.8 2.8 multiply_reduce_fusion.1
  357.3 3.3 convert_reduce_fusion.7
  370.8 51.4 %all-reduce.17.cloned.1.call-done = bf16[1024,1024]{1,0:T(8,128)(2,1)} async-done(((bf16[1024,1024]{1,0:T(8,128)(2,1)}), bf16[1024,1024]{1,0:T(8,128)(2,1)}) %all-reduce.17.cloned.1.call-update) | async-done | bytes 2097168 | tf_op jit(solution)/shard_map/psum | solution.py:154
  422.2 4.2 convert_reduce_fusion.2
  429.4 2.7 multiply_reduce_fusion
  432.9 2.7 copy-done.106
  435.6 4.0 convert_reduce_fusion.6
  441.0 3.7 fusion.71
  444.8 5.9 fusion.80
  450.7 45.6 %all-reduce.19.cloned.1.call-done = bf16[1024,1024]{1,0:T(8,128)(2,1)} async-done(((bf16[1024,1024]{1,0:T(8,128)(2,1)}), bf16[1024,1024]{1,0:T(8,128)(2,1)}) %all-reduce.19.cloned.1.call-update) | async-done | bytes 2097168 | tf_op jit(solution)/shard_map/psum | solution.py:95
  496.3 4.2 convert_reduce_fusion.1
  500.5 3.5 fusion.18
  504.1 3.2 multiply_reduce_fusion.2
  514.0 3.3 convert_reduce_fusion.8
  528.3 3.9 convolution_bitcast_fusion.4
  534.6 3.9 convolution_bitcast_fusion.5
  545.0 68.2 %all-reduce.21.cloned.1.call-done = (bf16[1024,1024]{1,0:T(8,128)(2,1)}, bf16[1024,1024]{1,0:T(8,128)(2,1)}) async-done(((bf16[1024,1024]{1,0:T(8,128)(2,1)}, bf16[1024,1024]{1,0:T(8,128)(2,1)}), (bf16[1024,1024]{1,0:T(8,128)(2,1)}, bf16[1024,1024]{1,0:T(8,128)(2,1)})) %all-reduce.21.cloned.1.call-update) | async-done | bytes 4194320 | tf_op jit(solution)/shard_map/psum | solution.py:71
  613.2 6.8 convert_reduce_fusion
  622.3 3.9 fusion.19
  627.3 2.7 pad_maximum_fusion.5
  645.2 5.7 convolution_bitcast_fusion.2
  653.4 4.1 pad_maximum_fusion
  657.6 5.5 convolution_bitcast_fusion.1
  665.5 4.1 pad_maximum_fusion.1
  669.6 9.3 reduce-scatter.68.cloned.1.call-done
  680.4 62.9 %reduce-scatter.70.cloned.1.call-done = f32[128,2]{1,0:T(8,128)} async-done(((f32[1024,2]{1,0:T(8,128)}), f32[128,2]{1,0:T(8,128)}) %reduce-scatter.70.cloned.1.call-update) | async-done | bytes 1040
  744.7 61.9 %reduce-scatter.58.cloned.1.call-done = f32[32,2]{1,0:T(8,128)} async-done(((f32[256,2]{1,0:T(8,128)}), f32[32,2]{1,0:T(8,128)}) %reduce-scatter.58.cloned.1.call-update) | async-done | bytes 272
  808.0 62.3 %reduce-scatter.56.cloned.1.call-done = f32[32,2]{1,0:T(8,128)} async-done(((f32[256,2]{1,0:T(8,128)}), f32[32,2]{1,0:T(8,128)}) %reduce-scatter.56.cloned.1.call-update) | async-done | bytes 272
  871.6 63.2 %reduce-scatter.66.cloned.1.call-done = f32[128,2]{1,0:T(8,128)} async-done(((f32[1024,2]{1,0:T(8,128)}), f32[128,2]{1,0:T(8,128)}) %reduce-scatter.66.cloned.1.call-update) | async-done | bytes 1040
  936.3 62.8 %reduce-scatter.64.cloned.1.call-done = f32[128,2]{1,0:T(8,128)} async-done(((f32[1024,2]{1,0:T(8,128)}), f32[128,2]{1,0:T(8,128)}) %reduce-scatter.64.cloned.1.call-update) | async-done | bytes 1040
  1000.6 63.0 %reduce-scatter.62.cloned.1.call-done = f32[128,2]{1,0:T(8,128)} async-done(((f32[1024,2]{1,0:T(8,128)}), f32[128,2]{1,0:T(8,128)}) %reduce-scatter.62.cloned.1.call-update) | async-done | bytes 1040
  1065.1 62.6 %reduce-scatter.60.cloned.1.call-done = f32[128,2]{1,0:T(8,128)} async-done(((f32[1024,2]{1,0:T(8,128)}), f32[128,2]{1,0:T(8,128)}) %reduce-scatter.60.cloned.1.call-update) | async-done | bytes 1040
  1129.2 4.9 add_add_fusion.4
  1134.1 58.1 %reduce-scatter.72.cloned.1.call-done = f32[128,2]{1,0:T(8,128)} async-done(((f32[1024,2]{1,0:T(8,128)}), f32[128,2]{1,0:T(8,128)}) %reduce-scatter.72.cloned.1.call-update) | async-done | bytes 1040
  1193.7 62.7 %reduce-scatter.54.cloned.1.call-done = f32[128,2]{1,0:T(8,128)} async-done(((f32[1024,2]{1,0:T(8,128)}), f32[128,2]{1,0:T(8,128)}) %reduce-scatter.54.cloned.1.call-update) | async-done | bytes 1040
  1257.8 63.1 %reduce-scatter.52.cloned.1.call-done = f32[128,2]{1,0:T(8,128)} async-done(((f32[1024,2]{1,0:T(8,128)}), f32[128,2]{1,0:T(8,128)}) %reduce-scatter.52.cloned.1.call-update) | async-done | bytes 1040
  1322.4 69.4 %reduce-scatter.46.cloned.1.call-done = f32[2,128,256]{2,1,0:T(8,128)} async-done(((f32[2,1024,256]{2,1,0:T(8,128)}), f32[2,128,256]{2,1,0:T(8,128)}) %reduce-scatter.46.cloned.1.call-update) | async-done | bytes 262160 | tf_op jit(solution)/shard_map/reduce_scatter | solution.py:250
  1391.8 70.9 %reduce-scatter.44.cloned.1.call-done = f32[2,128,256]{2,1,0:T(8,128)} async-done(((f32[2,1024,256]{2,1,0:T(8,128)}), f32[2,128,256]{2,1,0:T(8,128)}) %reduce-scatter.44.cloned.1.call-update) | async-done | bytes 262160 | tf_op jit(solution)/shard_map/reduce_scatter | solution.py:247
  1462.7 71.0 %reduce-scatter.42.cloned.1.call-done = f32[2,128,256]{2,1,0:T(8,128)} async-done(((f32[2,1024,256]{2,1,0:T(8,128)}), f32[2,128,256]{2,1,0:T(8,128)}) %reduce-scatter.42.cloned.1.call-update) | async-done | bytes 262160 | tf_op jit(solution)/shard_map/reduce_scatter | solution.py:246
  1533.7 71.2 %reduce-scatter.40.cloned.1.call-done = f32[2,128,256]{2,1,0:T(8,128)} async-done(((f32[2,1024,256]{2,1,0:T(8,128)}), f32[2,128,256]{2,1,0:T(8,128)}) %reduce-scatter.40.cloned.1.call-update) | async-done | bytes 262160 | tf_op jit(solution)/shard_map/reduce_scatter | solution.py:245
  1604.9 152.3 %reduce-scatter.48.cloned.1.call-done = f32[2,128,1024]{2,1,0:T(8,128)} async-done(((f32[2,1024,1024]{2,1,0:T(8,128)}), f32[2,128,1024]{2,1,0:T(8,128)}) %reduce-scatter.48.cloned.1.call-update) | async-done | bytes 1048592 | tf_op jit(solution)/shard_map/reduce_scatter | solution.py:255
  1757.2 152.6 %reduce-scatter.50.cloned.1.call-done = f32[2,128,1024]{2,1,0:T(8,128)} async-done(((f32[2,1024,1024]{2,1,0:T(8,128)}), f32[2,128,1024]{2,1,0:T(8,128)}) %reduce-scatter.50.cloned.1.call-update) | async-done | bytes 1048592 | tf_op jit(solution)/shard_map/reduce_scatter | solution.py:257
  (403 shorter events, 141.1 us)
Async XLA Ops:
  7.2 6.5 copy-start
  7.2 6.5 copy-start.85
  7.2 6.5 copy-start.93
  7.2 92.0 %all-reduce.9.cloned.1.call-start = ((), (), s32[]{:S(2)}) async-start(), calls=%async_computation.17 | async-start | bytes 4194304 | tf_op jit(solution)/shard_map/psum | solution.py:65
  8.1 6.4 copy-start.68
  8.1 7.8 copy-start.55
  20.7 6.5 copy-start.81
  20.7 6.7 copy-start.94
  33.9 4.8 copy-start.61
  45.0 129.3 %all-reduce.11.cloned.1.call-start = ((), (), s32[]{:S(2)}) async-start(), calls=%async_computation.18 | async-start | bytes 4194304 | tf_op jit(solution)/shard_map/psum | solution.py:71
  45.4 57.8 %copy-start.70 = (f32[1,1024]{1,0:T(1,128)}, f32[1,1024]{1,0:T(1,128)S(1)}, u32[]{:S(2)}) copy-start(f32[1,1024]{1,0:T(1,128)S(1)} %get-tuple-element.66) | copy-start | bytes 12292
  103.1 14.6 copy-start.76
  104.8 12.8 copy-start.45
  105.3 13.7 copy-start.98
  122.7 137.0 %all-reduce.13.cloned.1.call-start = ((), (), s32[]{:S(2)}) async-start(), calls=%async_computation.19 | async-start | bytes 4194304 | tf_op jit(solution)/shard_map/psum | solution.py:65
  123.2 85.2 %copy-start.74 = (f32[1,1024]{1,0:T(1,128)}, f32[1,1024]{1,0:T(1,128)S(1)}, u32[]{:S(2)}) copy-start(f32[1,1024]{1,0:T(1,128)S(1)} %get-tuple-element.61) | copy-start | bytes 12292
  201.8 4.2 copy-start.25
  208.1 132.4 %all-reduce.15.cloned.1.call-start = ((), (), s32[]{:S(2)}) async-start(), calls=%async_computation.20 | async-start | bytes 4194304 | tf_op jit(solution)/shard_map/psum | solution.py:95
  263.4 16.4 copy-start.3
  267.1 12.7 copy-start.47
  267.1 12.7 copy-start.99
  288.9 133.2 %all-reduce.17.cloned.1.call-start = ((), (), s32[]{:S(2)}) async-start(), calls=%async_computation.21 | async-start | bytes 4194304 | tf_op jit(solution)/shard_map/psum | solution.py:154
  340.5 4.2 copy-start.4
  340.5 4.7 copy-start.13
  370.6 125.7 %all-reduce.19.cloned.1.call-start = ((), (), s32[]{:S(2)}) async-start(), calls=%async_computation.22 | async-start | bytes 4194304 | tf_op jit(solution)/shard_map/psum | solution.py:95
  422.2 4.2 copy-start.2
  422.2 4.7 copy-start.10
  429.4 6.2 copy-start.106
  432.2 7.4 copy-start.14
  435.6 5.4 copy-start.97
  444.7 168.5 %all-reduce.21.cloned.1.call-start = ((), (), s32[]{:S(2)}) async-start(), calls=%async_computation.40 | async-start | bytes 8388608 | tf_op jit(solution)/shard_map/psum | solution.py:71
  444.7 51.6 %copy-start.67 = (f32[1024]{0:T(1024)S(1)}, f32[1024]{0:T(1024)}, u32[]{:S(2)}) copy-start(f32[1024]{0:T(1024)} %copy-done.66) | copy-start | bytes 12292
  444.8 51.6 %copy-start.71 = (f32[1,1024]{1,0:T(1,128)S(1)}, f32[1,1024]{1,0:T(1,128)}, u32[]{:S(2)}) copy-start(f32[1,1024]{1,0:T(1,128)} %copy-done.70) | copy-start | bytes 12292
  450.7 49.8 %copy-start.77 = (f32[1024]{0:T(1024)S(1)}, f32[1024]{0:T(1024)}, u32[]{:S(2)}) copy-start(f32[1024]{0:T(1024)} %copy-done.76) | copy-start | bytes 12292
  450.7 49.8 %copy-start.73 = (f32[1024]{0:T(1024)S(1)}, f32[1024]{0:T(1024)}, u32[]{:S(2)}) copy-start(f32[1024]{0:T(1024)} %copy-done.72) | copy-start | bytes 12292
  504.1 5.1 copy-start.26
  509.2 4.8 copy-start.79
  527.3 6.1 copy-start.84
  527.3 7.3 copy-start.19
  527.3 151.6 %reduce-scatter.68.cloned.1.call-start = ((), (), s32[]{:S(2)}) async-start(), calls=%async_computation.37 | async-start | bytes 589824
  533.3 209.9 %reduce-scatter.70.cloned.1.call-start = ((), (), s32[]{:S(2)}) async-start(), calls=%async_computation.38 | async-start | bytes 589824
  534.5 78.7 %copy-start.69 = (f32[1,1024]{1,0:T(1,128)S(1)}, f32[1,1024]{1,0:T(1,128)}, u32[]{:S(2)}) copy-start(f32[1,1024]{1,0:T(1,128)} %copy-done.68) | copy-start | bytes 12292
  534.5 78.7 %copy-start.75 = (f32[1,1024]{1,0:T(1,128)S(1)}, f32[1,1024]{1,0:T(1,128)}, u32[]{:S(2)}) copy-start(f32[1,1024]{1,0:T(1,128)} %copy-done.74) | copy-start | bytes 12292
  534.5 78.7 %copy-start.80 = (f32[1,1024]{1,0:T(1,128)S(1)}, f32[1,1024]{1,0:T(1,128)}, u32[]{:S(2)}) copy-start(f32[1,1024]{1,0:T(1,128)} %get-tuple-element.59) | copy-start | bytes 12292
  534.5 272.1 %reduce-scatter.58.cloned.1.call-start = ((), (), s32[]{:S(2)}) async-start(), calls=%async_computation.32 | async-start | bytes 147456
  539.5 330.8 %reduce-scatter.56.cloned.1.call-start = ((), (), s32[]{:S(2)}) async-start(), calls=%async_computation.31 | async-start | bytes 147456
  540.4 394.4 %reduce-scatter.66.cloned.1.call-start = ((), (), s32[]{:S(2)}) async-start(), calls=%async_computation.36 | async-start | bytes 589824
  541.5 457.6 %reduce-scatter.64.cloned.1.call-start = ((), (), s32[]{:S(2)}) async-start(), calls=%async_computation.35 | async-start | bytes 589824
  542.6 521.0 %reduce-scatter.62.cloned.1.call-start = ((), (), s32[]{:S(2)}) async-start(), calls=%async_computation.34 | async-start | bytes 589824
  543.8 584.0 %reduce-scatter.60.cloned.1.call-start = ((), (), s32[]{:S(2)}) async-start(), calls=%async_computation.33 | async-start | bytes 589824
  544.9 647.3 %reduce-scatter.72.cloned.1.call-start = ((), (), s32[]{:S(2)}) async-start(), calls=%async_computation.39 | async-start | bytes 589824
  620.0 7.3 copy-start.27
  621.1 635.3 %reduce-scatter.54.cloned.1.call-start = ((), (), s32[]{:S(2)}) async-start(), calls=%async_computation.30 | async-start | bytes 589824
  622.2 698.7 %reduce-scatter.52.cloned.1.call-start = ((), (), s32[]{:S(2)}) async-start(), calls=%async_computation.29 | async-start | bytes 589824
  627.3 764.6 %reduce-scatter.46.cloned.1.call-start = ((), (), s32[]{:S(2)}) async-start(), calls=%async_computation.26 | async-start | bytes 2359296 | tf_op jit(solution)/shard_map/reduce_scatter | solution.py:250
  630.1 832.6 %reduce-scatter.44.cloned.1.call-start = ((), (), s32[]{:S(2)}) async-start(), calls=%async_computation.25 | async-start | bytes 2359296 | tf_op jit(solution)/shard_map/reduce_scatter | solution.py:247
  635.1 898.6 %reduce-scatter.42.cloned.1.call-start = ((), (), s32[]{:S(2)}) async-start(), calls=%async_computation.24 | async-start | bytes 2359296 | tf_op jit(solution)/shard_map/reduce_scatter | solution.py:246
  640.0 964.9 %reduce-scatter.40.cloned.1.call-start = ((), (), s32[]{:S(2)}) async-start(), calls=%async_computation.23 | async-start | bytes 2359296 | tf_op jit(solution)/shard_map/reduce_scatter | solution.py:245
  644.9 1112.3 %reduce-scatter.48.cloned.1.call-start = ((), (), s32[]{:S(2)}) async-start(), calls=%async_computation.27 | async-start | bytes 9437184 | tf_op jit(solution)/shard_map/reduce_scatter | solution.py:255
  645.1 5.8 copy-start.46
  645.2 5.8 copy-start.104
  657.5 1252.3 %reduce-scatter.50.cloned.1.call-start = ((), (), s32[]{:S(2)}) async-start(), calls=%async_computation.28 | async-start | bytes 9437184 | tf_op jit(solution)/shard_map/reduce_scatter | solution.py:257
  657.5 5.5 copy-start.29
  657.5 5.5 copy-start.102
  (68 other events, 168.6 us)
Sparse Core Ops, SparseCore 0:
  45.1 54.0 all-reduce.8
  122.8 51.4 all-reduce.10
  208.3 51.4 all-reduce.12
  289.1 51.4 all-reduce.14
  370.7 51.4 all-reduce.16
  444.8 51.4 all-reduce.18
  527.4 85.7 all-reduce.20
  616.9 61.9 reduce-scatter.67
  682.3 60.9 reduce-scatter.69
  746.8 59.7 reduce-scatter.57
  810.3 59.8 reduce-scatter.55
  873.8 60.9 reduce-scatter.65
  938.2 60.9 reduce-scatter.63
  1002.7 60.8 reduce-scatter.61
  1066.8 60.8 reduce-scatter.59
  1131.3 60.8 reduce-scatter.71
  1195.4 60.9 reduce-scatter.53
  1259.9 60.9 reduce-scatter.51
  1325.0 66.7 reduce-scatter.45
  1395.8 66.9 reduce-scatter.43
  1466.9 66.8 reduce-scatter.41
  1537.8 67.0 reduce-scatter.39
  1609.1 148.0 reduce-scatter.47
  1761.7 148.0 reduce-scatter.49
where the time goes:
time: 1930 us; the launch traced here: 1920 us
  waiting for transfers between devices  1590 us (82%)
  matrix products  139 us (7%)
  other arithmetic  88.3 us (5%)
  local copies, waits for them, and re-layouts  83.1 us (4%)
    unnamed x35, waiting for transfers between devices  632 us
    reduce_scatter x1, waiting for transfers between devices, per_device(): lax.psum_scatter(stacked[14], 'dp', scatter_dimension=1, tiled=True)  153 us
    reduce_scatter x1, waiting for transfers between devices, per_device(): lax.psum_scatter(stacked[12], 'dp', scatter_dimension=1, tiled=True)  152 us
    psum x2, waiting for transfers between devices, forward_layer(): fed = lax.psum(partial_feed.astype(jnp.bfloat16), 'mp').astype(jnp.float32)  119 us
    psum x2, waiting for transfers between devices, forward_layer(): lax.psum(partial_out.astype(jnp.bfloat16), 'mp').astype(jnp.float32)  101 us
    psum x2, waiting for transfers between devices, backward_layer(): lax.psum(partial_normed2.astype(jnp.bfloat16), 'mp').astype(jnp.float32)  97.2 us
    reduce_scatter x1, waiting for transfers between devices, per_device(): lax.psum_scatter(stacked[2], 'dp', scatter_dimension=1, tiled=True)  71.2 us
    reduce_scatter x1, waiting for transfers between devices, per_device(): lax.psum_scatter(stacked[3], 'dp', scatter_dimension=1, tiled=True)  71 us
  transfers between devices with their start and end apart: 24, of which 24 were waited for; matrix products, arithmetic and copies ran while one was open for 5% of the time, Pallas kernels for 0%

commit v1 on v0

v1 whole, which is shorter than its diff:
```python
import functools
import math

import jax
import jax.numpy as jnp
from jax import lax
from jax.experimental import pallas as pl
from jax.experimental.pallas import tpu as pltpu
from jax.sharding import PartitionSpec as P

HD = 64
EPSILON = 1e-06
MASKED = -1e30
F32 = jnp.float32
BF16 = jnp.bfloat16
CONTRACT_LAST = (((1,), (1,)), ((), ()))
CONTRACT_ROWS = (((0,), (0,)), ((), ()))
VMEM_LIMIT = 56 * 1024 * 1024
SAMPLE = 2


def dot(a, b):
    return jnp.dot(a, b, preferred_element_type=F32)


def dot_last(a, b):
    return lax.dot_general(a, b, CONTRACT_LAST, preferred_element_type=F32)


def dot_rows(a, b):
    return lax.dot_general(a, b, CONTRACT_ROWS, preferred_element_type=F32)


def normalise(values):
    center = values - jnp.mean(values, axis=-1, keepdims=True)
    spread = jnp.mean(center * center, axis=-1, keepdims=True)
    factor = lax.rsqrt(spread + EPSILON)
    return center * factor, factor


def norm_back(hat, factor, gain, grad):
    inner = grad * gain
    first = jnp.mean(inner, axis=-1, keepdims=True)
    second = jnp.mean(inner * hat, axis=-1, keepdims=True)
    return factor * (inner - first - hat * second)


def column_sum(values):
    return jnp.sum(values, axis=0, keepdims=True)


def fetch(plan, sems):
    copies = []
    for index, (source, target) in enumerate(plan):
        copy = pltpu.make_async_copy(source, target, sems.at[index])
        copy.start()
        copies.append(copy)
    return copies


def residual(values, scale, mine, theirs, bias):
    return values + scale * (mine.astype(F32) + theirs.astype(F32) + bias)


def attend_forward(layer, *refs):
    if layer == 0:
        source, refs = refs[0], refs[1:]
    else:
        (middle, mine, theirs, feed_scale, down_bias), refs = refs[:5], refs[5:]
    (mask, gain, shift, query_bias, value_bias) = refs[:5]
    (wq0, wq1, wk0, wk1, wv0, wv1, wo0, wo1) = refs[5:13]
    (current, normed_out, query_out, key_out, value_out, probs_out, mixed_out, part) = refs[13:21]
    wq, wk, wv, wo, sems = refs[21:]
    half = wq0.shape[2]
    now = slice(layer, layer + 1)
    plan = []
    for own, other, target in ((wq0, wq1, wq), (wk0, wk1, wk), (wv0, wv1, wv), (wo0, wo1, wo)):
        plan.append((own.at[layer], target.at[:, :half]))
        plan.append((other.at[layer], target.at[:, half:]))
    copies = fetch(plan, sems)
    if layer == 0:
        values = source[...].astype(F32)
    else:
        before = slice(layer - 1, layer)
        values = residual(
            middle[...], feed_scale[before], mine[...], theirs[...], down_bias[before]
        )
    current[...] = values
    hat, _ = normalise(values)
    normed = (hat * gain[now] + shift[now]).astype(BF16)
    normed_out[...] = normed
    copies[0].wait()
    copies[1].wait()
    query_out[...] = (dot(normed, wq[...]) + query_bias[now]).astype(BF16)
    copies[2].wait()
    copies[3].wait()
    key_out[...] = dot(normed, wk[...]).astype(BF16)
    copies[4].wait()
    copies[5].wait()
    value_out[...] = (dot(normed, wv[...]) + value_bias[now]).astype(BF16)
    pairs = 2 * half // (2 * HD)
    lane = lax.broadcasted_iota(jnp.int32, (values.shape[0], 2 * HD), 1)
    scale = jnp.asarray(HD ** (-0.5), BF16)
    blocked = mask[...]
    for pair in range(pairs):
        cols = slice(pair * 2 * HD, (pair + 1) * 2 * HD)
        query = query_out[:, cols] * scale
        key = key_out[:, cols]
        value = value_out[:, cols]
        mixed = []
        for side in range(2):
            lanes = (lane < HD) if side == 0 else (lane >= HD)
            scores = dot_last(jnp.where(lanes, query, jnp.zeros_like(query)), key) + blocked
            top = jnp.max(scores, axis=-1, keepdims=True)
            weights = jnp.exp(scores - top)
            total = jnp.sum(weights, axis=-1, keepdims=True)
            probs = (weights * (1.0 / total)).astype(BF16)
            probs_out[2 * pair + side] = probs
            mixed.append(dot(probs, value))
        mixed_out[:, cols] = jnp.where(lane < HD, mixed[0], mixed[1]).astype(BF16)
    copies[6].wait()
    copies[7].wait()
    part[...] = dot_last(mixed_out[...], wo[...]).astype(BF16)


def feed_forward(layer, *refs):
    (current, mine, theirs, attend_scale, out_bias, gain, shift, up_bias) = refs[:8]
    (wu0, wu1, wd0, wd1) = refs[8:12]
    (middle, normed_out, act0, act1, slope0, slope1, part) = refs[12:19]
    wu, wd, sems = refs[19:]
    half = wu0.shape[2]
    width = half // 2
    now = slice(layer, layer + 1)
    plan = []
    for index in range(4):
        cols = slice((index % 2) * width, (index % 2 + 1) * width)
        plan.append(((wu0, wu1)[index // 2].at[layer, :, cols], wu.at[index]))
    for index in range(4):
        cols = slice((index % 2) * width, (index % 2 + 1) * width)
        plan.append(((wd0, wd1)[index // 2].at[layer, :, cols], wd.at[index]))
    copies = fetch(plan, sems)
    values = residual(current[...], attend_scale[now], mine[...], theirs[...], out_bias[now])
    middle[...] = values
    hat, _ = normalise(values)
    normed = (hat * gain[now] + shift[now]).astype(BF16)
    normed_out[...] = normed
    total = None
    for index in range(4):
        copies[index].wait()
        before = dot(normed, wu[index]) + up_bias[now, index * width : (index + 1) * width]
        lower = 0.5 * (1.0 + lax.erf(before * math.sqrt(0.5)))
        active = (before * lower).astype(BF16)
        bell = jnp.exp(-0.5 * before * before) * (1.0 / math.sqrt(2.0 * math.pi))
        slope = (lower + before * bell).astype(BF16)
        cols = slice((index % 2) * width, (index % 2 + 1) * width)
        (act0, act1)[index // 2][:, cols] = active
        (slope0, slope1)[index // 2][:, cols] = slope
        copies[4 + index].wait()
        term = dot_last(active, wd[index])
        total = term if total is None else total + term
    part[...] = total.astype(BF16)


def finish_forward(layer, middle, mine, theirs, feed_scale, down_bias, result):
    now = slice(layer, layer + 1)
    result[...] = residual(
        middle[...], feed_scale[now], mine[...], theirs[...], down_bias[now]
    ).astype(BF16)


def feed_backward(layer, last, *refs):
    if last:
        source, refs = refs[0], refs[1:]
    else:
        (after, deep, deep_mine, deep_theirs, deep_gain), refs = refs[:5], refs[5:]
    (fed_mine, fed_theirs, feed_scale, down_bias, slope0, slope1) = refs[:6]
    (wu0, wu1, wd0, wd1) = refs[6:10]
    (grad_out, grad_fed_out, before0, before1, part, sums, wide_sums) = refs[10:17]
    wu, wd, sems = refs[17:]
    half = wu0.shape[2]
    width = half // 2
    now = slice(layer, layer + 1)
    plan = []
    for index in range(4):
        cols = slice((index % 2) * width, (index % 2 + 1) * width)
        plan.append(((wd0, wd1)[index // 2].at[layer, :, cols], wd.at[index]))
    for index in range(4):
        cols = slice((index % 2) * width, (index % 2 + 1) * width)
        plan.append(((wu0, wu1)[index // 2].at[layer, :, cols], wu.at[index]))
    copies = fetch(plan, sems)
    if last:
        grad = source[...].astype(F32)
        zero = jnp.zeros((1, grad.shape[1]), F32)
        sums[2:3] = zero
        sums[3:4] = zero
    else:
        hat, factor = normalise(deep[...])
        grad_normed = deep_mine[...].astype(F32) + deep_theirs[...].astype(F32)
        grad = after[...] + norm_back(hat, factor, deep_gain[layer + 1 : layer + 2], grad_normed)
        sums[2:3] = column_sum(grad_normed * hat)
        sums[3:4] = column_sum(grad_normed)
    grad_out[...] = grad
    scaled = feed_scale[now] * grad
    grad_fed = scaled.astype(BF16)
    grad_fed_out[...] = grad_fed
    sums[0:1] = column_sum(scaled)
    fed = fed_mine[...].astype(F32) + fed_theirs[...].astype(F32)
    sums[1:2] = column_sum(grad * (fed + down_bias[now]))
    total = None
    for index in range(4):
        cols = slice((index % 2) * width, (index % 2 + 1) * width)
        copies[index].wait()
        grad_active = dot(grad_fed, wd[index])
        slope = (slope0, slope1)[index // 2][:, cols].astype(F32)
        before = (grad_active * slope).astype(BF16)
        (before0, before1)[index // 2][:, cols] = before
        wide_sums[:, index * width : (index + 1) * width] = column_sum(before.astype(F32))
        copies[4 + index].wait()
        term = dot_last(before, wu[index])
        total = term if total is None else total + term
    part[...] = total.astype(BF16)


def attend_backward(layer, *refs):
    (grad_in, middle, mine, theirs, gain) = refs[:5]
    (att_mine, att_theirs, attend_scale, out_bias) = refs[5:9]
    (query_in, key_in, value_in, probs_in) = refs[9:13]
    (wq0, wq1, wk0, wk1, wv0, wv1, wo0, wo1) = refs[13:21]
    (grad_out, grad_att_out, gq, gk, gv, part, sums, wide_sums) = refs[21:29]
    wq, wk, wv, wo, mixed_scratch, sems = refs[29:]
    half = wq0.shape[2]
    now = slice(layer, layer + 1)
    plan = []
    for own, other, target in ((wo0, wo1, wo), (wq0, wq1, wq), (wk0, wk1, wk), (wv0, wv1, wv)):
        plan.append((own.at[layer], target.at[:, :half]))
        plan.append((other.at[layer], target.at[:, half:]))
    copies = fetch(plan, sems)
    hat, factor = normalise(middle[...])
    grad_normed = mine[...].astype(F32) + theirs[...].astype(F32)
    grad = grad_in[...] + norm_back(hat, factor, gain[now], grad_normed)
    grad_out[...] = grad
    scaled = attend_scale[now] * grad
    grad_att = scaled.astype(BF16)
    grad_att_out[...] = grad_att
    sums[0:1] = column_sum(scaled)
    attended = att_mine[...].astype(F32) + att_theirs[...].astype(F32)
    sums[1:2] = column_sum(grad * (attended + out_bias[now]))
    sums[2:3] = column_sum(grad_normed * hat)
    sums[3:4] = column_sum(grad_normed)
    copies[0].wait()
    copies[1].wait()
    mixed_scratch[...] = dot(grad_att, wo[...]).astype(BF16)
    pairs = 2 * half // (2 * HD)
    lane = lax.broadcasted_iota(jnp.int32, (grad.shape[0], 2 * HD), 1)
    scale = HD ** (-0.5)
    for pair in range(pairs):
        cols = slice(pair * 2 * HD, (pair + 1) * 2 * HD)
        query = query_in[:, cols]
        key = key_in[:, cols]
        value = value_in[:, cols]
        mixed = mixed_scratch[:, cols]
        found = []
        for side in range(2):
            lanes = (lane < HD) if side == 0 else (lane >= HD)
            probs_low = probs_in[2 * pair + side]
            probs = probs_low.astype(F32)
            grad_probs = dot_last(jnp.where(lanes, mixed, jnp.zeros_like(mixed)), value)
            weighted = probs * grad_probs
            row = jnp.sum(weighted, axis=-1, keepdims=True)
            grad_scores = (weighted - probs * row).astype(BF16)
            found.append(
                (dot(grad_scores, key), dot_rows(grad_scores, query), dot_rows(probs_low, mixed))
            )
        first = lane < HD
        gq[:, cols] = (jnp.where(first, found[0][0], found[1][0]) * scale).astype(BF16)
        gk[:, cols] = (jnp.where(first, found[0][1], found[1][1]) * scale).astype(BF16)
        gv[:, cols] = jnp.where(first, found[0][2], found[1][2]).astype(BF16)
    wide_sums[0:1] = column_sum(gq[...].astype(F32))
    wide_sums[1:2] = column_sum(gv[...].astype(F32))
    for copy in copies[2:]:
        copy.wait()
    total = dot_last(gq[...], wq[...]) + dot_last(gk[...], wk[...]) + dot_last(gv[...], wv[...])
    part[...] = total.astype(BF16)


def finish_backward(after, deep, mine, theirs, gain, grad_out, sums):
    hat, factor = normalise(deep[...])
    grad_normed = mine[...].astype(F32) + theirs[...].astype(F32)
    grad_out[...] = after[...] + norm_back(hat, factor, gain[0:1], grad_normed)
    sums[0:1] = column_sum(grad_normed * hat)
    sums[1:2] = column_sum(grad_normed)


def weight_grad(chunks, count, has_other, places, *refs):
    lefts = refs[: 2 * count]
    rights = refs[2 * count : 4 * count]
    refs = refs[4 * count :]
    if has_other:
        others, refs = refs[:count], refs[count:]
    outs, turned = refs[:count], refs[count:]
    step = pl.program_id(0)
    tokens = lefts[0].shape[0]

    @pl.when(step == 0)
    def _():
        for index in range(count):
            for sample in range(2):
                turned[index][:, sample * tokens : (sample + 1) * tokens] = lefts[
                    2 * index + sample
                ][...].T

    for index in range(count):
        right = jnp.concatenate([rights[2 * index][...], rights[2 * index + 1][...]], axis=0)
        product = dot(turned[index][...], right)
        rows = product.shape[0] // chunks
        for chunk in range(chunks):
            at = pl.multiple_of(places[index, chunk] * rows, rows)
            block = product[chunk * rows : (chunk + 1) * rows]
            if has_other:
                block = block + others[index][pl.ds(at, rows), :].astype(F32)
            outs[index][pl.ds(at, rows), :] = block.astype(BF16)


def whole(array):
    rank = len(array.shape)
    return pl.BlockSpec(array.shape, lambda i, rank=rank: (0,) * rank)


def one_of(array, index):
    rank = len(array.shape)
    return pl.BlockSpec(
        (None,) + array.shape[1:], lambda i, index=index, rank=rank: (index,) + (0,) * (rank - 1)
    )


ANYWHERE = pl.BlockSpec(memory_space=pl.ANY)


def run(body, inputs, specs, outputs, scratch, name, flops):
    shapes = [jax.ShapeDtypeStruct(shape, kind) for shape, kind in outputs]
    moved = sum(math.prod(shape) * jnp.dtype(kind).itemsize for shape, kind in outputs)
    moved += sum(
        math.prod(value.shape) * value.dtype.itemsize // value.shape[0]
        for value in inputs
    )
    return pl.pallas_call(
        body,
        out_shape=shapes,
        grid=(1,),
        in_specs=specs,
        out_specs=[whole(shape) for shape in shapes],
        scratch_shapes=scratch,
        compiler_params=pltpu.CompilerParams(vmem_limit_bytes=VMEM_LIMIT),
        cost_estimate=pl.CostEstimate(flops=flops, bytes_accessed=moved, transcendentals=0),
        name=name,
    )(*inputs)


def weight_grads(pairs, places, others, blocks, name):
    count = len(pairs)
    inputs, specs = [], []
    for lefts, _ in pairs:
        for left in lefts:
            inputs.append(left)
            specs.append(pl.BlockSpec(left.shape, lambda j, table: (0, 0)))
    for _, rights in pairs:
        for right, start in rights:
            width = WIDTHS(right, start) // blocks
            inputs.append(right)
            first = start[0] // width
            specs.append(
                pl.BlockSpec((right.shape[0], width), lambda j, table, first=first: (0, first + j))
            )
    shapes, out_specs, scratch = [], [], []
    for lefts, rights in pairs:
        width = WIDTHS(*rights[0])
        rows = lefts[0].shape[1]
        shapes.append(jax.ShapeDtypeStruct((rows, width), BF16))
        out_specs.append(pl.BlockSpec((rows, width // blocks), lambda j, table: (0, j)))
        scratch.append(pltpu.VMEM((rows, 2 * lefts[0].shape[0]), BF16))
    if others is not None:
        for other, spec in zip(others, out_specs):
            inputs.append(other)
            specs.append(spec)
    tokens = 2 * pairs[0][0][0].shape[0]
    flops = sum(2 * tokens * math.prod(shape.shape) for shape in shapes)
    moved = sum(2 * math.prod(shape.shape) for shape in shapes) * (1 if others is None else 2)
    moved += sum(value.size * 2 for value in inputs[: 4 * count])
    return pl.pallas_call(
        functools.partial(weight_grad, places.shape[1], count, others is not None),
        out_shape=shapes,
        grid_spec=pltpu.PrefetchScalarGridSpec(
            num_scalar_prefetch=1,
            grid=(blocks,),
            in_specs=specs,
            out_specs=out_specs,
            scratch_shapes=scratch,
        ),
        compiler_params=pltpu.CompilerParams(vmem_limit_bytes=VMEM_LIMIT),
        cost_estimate=pl.CostEstimate(flops=flops, bytes_accessed=moved, transcendentals=0),
        name=name,
    )(places, *inputs)


def WIDTHS(right, span):
    return span[1] - span[0]


def ring_order(n):
    return list(range(0, n, 2)) + list(range(n - 1, 0, -2))


def ring_scatter(clockwise, counter, n):
    order = ring_order(n)
    forward = [(order[i], order[(i + 1) % n]) for i in range(n)]
    backward = [(b, a) for a, b in forward]
    rows = clockwise.shape[0] // n
    one, two = clockwise[:rows], counter[:rows]
    for step in range(n - 1):
        one = lax.ppermute(one, "dp", forward)
        two = lax.ppermute(two, "dp", backward)
        span = slice((step + 1) * rows, (step + 2) * rows)
        one = one.astype(F32) + clockwise[span].astype(F32)
        two = two.astype(F32) + counter[span].astype(F32)
        if step < n - 2:
            one, two = one.astype(BF16), two.astype(BF16)
    return one, two


def small_scatter(packed, n):
    me = lax.axis_index("dp")
    turned = jnp.take(packed, (me + jnp.arange(n)) % n, axis=0)
    total = turned[0]
    for shift in range(1, n):
        total = total + lax.ppermute(
            turned[shift], "dp", [(i, (i + shift) % n) for i in range(n)]
        )
    return total


def per_device(
    n,
    activations,
    segments,
    first_gain,
    first_shift,
    query_weight,
    key_weight,
    value_weight,
    query_bias,
    value_bias,
    out_weight,
    out_bias,
    attend_scale,
    second_gain,
    second_shift,
    up_weight,
    up_bias,
    down_weight,
    down_bias,
    feed_scale,
    cotangent,
):
    rows, slots, width = activations.shape
    layers = first_gain.shape[0]
    mp = lax.axis_index("mp")
    core = mp % 2
    mine_rows = rows // 2
    tokens = mine_rows // SAMPLE * slots
    heads_half = query_weight.shape[2]
    hidden_half = up_weight.shape[2]
    features = 2 * heads_half
    hidden = 2 * hidden_half
    heads = features // HD
    samples = range(SAMPLE)
    ring = n <= 8 and n % 2 == 0

    def swap_core(value):
        return lax.ppermute(value, "mp", [(i, i ^ 1) for i in range(4)])

    def swap_x(value):
        return lax.ppermute(value, "mp", [(i, i ^ 2) for i in range(4)])

    biases = jnp.concatenate([query_bias, value_bias, up_bias], axis=1)
    wq1, wk1, wv1 = swap_core(query_weight), swap_core(key_weight), swap_core(value_weight)
    biases_other = swap_core(biases)
    wo1 = swap_core(out_weight)
    wu1, wd1 = swap_core(up_weight), swap_core(down_weight)
    both = jnp.concatenate([biases, biases_other], axis=1)
    span = heads_half * 2 + hidden_half
    query_bias_all = jnp.concatenate([both[:, :heads_half], both[:, span : span + heads_half]], 1)
    value_bias_all = jnp.concatenate(
        [both[:, heads_half:features], both[:, span + heads_half : span + features]], 1
    )
    up_bias_all = jnp.concatenate([both[:, features:span], both[:, span + features :]], 1)
    attend_weights = [query_weight, wq1, key_weight, wk1, value_weight, wv1, out_weight, wo1]
    feed_weights = [up_weight, wu1, down_weight, wd1]

    def own_rows(value):
        start = (core * mine_rows,) + (0,) * (value.ndim - 1)
        return lax.dynamic_slice(value, start, (mine_rows,) + value.shape[1:])

    own_segments = own_rows(segments)
    same = own_segments[:, :, None] == own_segments[:, None, :]
    masks = jnp.where(same, 0.0, MASKED).astype(F32)
    own_input = own_rows(activations)
    own_cotangent = own_rows(cotangent)
    assert tokens == slots

    attend_scratch = [
        pltpu.VMEM((width, features), BF16),
        pltpu.VMEM((width, features), BF16),
        pltpu.VMEM((width, features), BF16),
        pltpu.VMEM((width, features), BF16),
    ]
    feed_scratch = [
        pltpu.VMEM((4, width, hidden_half // 2), BF16),
        pltpu.VMEM((4, width, hidden_half // 2), BF16),
        pltpu.SemaphoreType.DMA((8,)),
    ]
    act = ((tokens, width), BF16)
    state = ((tokens, width), F32)
    head = ((tokens, features), BF16)
    hid = ((tokens, hidden_half), BF16)
    probs_shape = ((heads, slots, slots), BF16)
    attend_flops = 2 * tokens * width * features * 4 + 4 * tokens * slots * heads * 128
    feed_flops = 4 * tokens * width * hidden

    saved = [[None] * SAMPLE for _ in range(layers)]
    state_now = [None] * SAMPLE
    fed = [None] * SAMPLE
    for layer in range(layers):
        parts = []
        for m in samples:
            if layer == 0:
                inputs, specs = [own_input], [one_of(own_input, m)]
            else:
                inputs = [state_now[m], fed[m][0], fed[m][1], feed_scale, down_bias]
                specs = [whole(v) for v in inputs]
                inputs[3:5] = [feed_scale, down_bias]
            more = [first_gain, first_shift, query_bias_all, value_bias_all]
            inputs = inputs + [masks] + more + attend_weights
            specs = specs + [one_of(masks, m)] + [whole(v) for v in more] + [ANYWHERE] * 8
            outs = run(
                functools.partial(attend_forward, layer),
                inputs,
                specs,
                [state, act, head, head, head, probs_shape, head, act],
                attend_scratch + [pltpu.SemaphoreType.DMA((8,))],
                "attend_forward",
                attend_flops,
            )
            kept = dict(zip(("current", "normed", "q", "k", "v", "probs", "mixed"), outs))
            saved[layer][m] = kept
            kept["att"] = (outs[7], swap_x(outs[7]))
        for m in samples:
            kept = saved[layer][m]
            vectors = [attend_scale, out_bias, second_gain, second_shift, up_bias_all]
            inputs = [kept["current"], *kept["att"]] + vectors
            outs = run(
                functools.partial(feed_forward, layer),
                inputs + feed_weights,
                [whole(v) for v in inputs] + [ANYWHERE] * 4,
                [state, act, hid, hid, hid, hid, act],
                feed_scratch,
                "feed_forward",
                feed_flops,
            )
            kept.update(zip(("middle", "normed2", "act0", "act1", "slope0", "slope1"), outs))
            state_now[m] = outs[0]
            fed[m] = kept["fed"] = (outs[6], swap_x(outs[6]))

    results = []
    for m in samples:
        inputs = [state_now[m], *fed[m], feed_scale, down_bias]
        results.append(
            run(
                functools.partial(finish_forward, layers - 1),
                inputs,
                [whole(v) for v in inputs],
                [act],
                [],
                "finish_forward",
                tokens * width,
            )[0]
        )

    if ring:
        me = lax.axis_index("dp")
        place = jnp.where(me % 2 == 0, me // 2, (2 * n - 1 - me) // 2)
        chunk = jnp.arange(n)
        chunk_place = jnp.where(chunk % 2 == 0, chunk // 2, (2 * n - 1 - chunk) // 2)
        table_one = (place - 1 - chunk_place) % n
        table_two = (chunk_place - place - 1) % n
    else:
        table_one = table_two = jnp.arange(8)
    places_feed = jnp.stack([table_one, table_two]).astype(jnp.int32)
    places_attend = jnp.stack([table_one, table_one, table_two, table_two]).astype(jnp.int32)

    def reduce_pair(one, two):
        if ring:
            return ring_scatter(one, two, n)
        both_now = jnp.concatenate([one, two], axis=1).astype(F32)
        done = lax.psum_scatter(both_now, "dp", scatter_dimension=0, tiled=True)
        return done[:, : one.shape[1]], done[:, one.shape[1] :]

    grads = [None] * layers
    smalls = [None] * layers
    late_sums = [None] * layers
    carry = [None] * SAMPLE
    for layer in reversed(range(layers)):
        last = layer == layers - 1
        feed_sums, attend_sums = [], []
        for m in samples:
            kept = saved[layer][m]
            if last:
                inputs, specs = [own_cotangent], [one_of(own_cotangent, m)]
            else:
                inputs = [*carry[m], first_gain]
                specs = [whole(v) for v in inputs]
            more = [*kept["fed"], feed_scale, down_bias, kept["slope0"], kept["slope1"]]
            outs = run(
                functools.partial(feed_backward, layer, last),
                inputs + more + feed_weights,
                specs + [whole(v) for v in more] + [ANYWHERE] * 4,
                [state, act, hid, hid, act, ((4, width), F32), ((1, hidden), F32)],
                feed_scratch,
                "feed_backward",
                feed_flops,
            )
            kept.update(zip(("grad", "grad_fed", "before0", "before1"), outs))
            kept["n2"] = (outs[4], swap_x(outs[4]))
            feed_sums.append(outs[5:])
        kept = saved[layer]

        def spans(name, length, offset=0):
            return [(kept[m][name], (offset, offset + length)) for m in samples]

        lefts_up = [kept[m]["normed2"] for m in samples]
        lefts_down = [kept[m]["grad_fed"] for m in samples]
        given = weight_grads(
            [(lefts_up, spans("before1", hidden_half)), (lefts_down, spans("act1", hidden_half))],
            places_feed,
            None,
            4,
            "feed_grads_given",
        )
        taken = [swap_core(value) for value in given]
        up_part, down_part = weight_grads(
            [(lefts_up, spans("before0", hidden_half)), (lefts_down, spans("act0", hidden_half))],
            places_feed,
            taken,
            4,
            "feed_grads",
        )
        up_grad, down_grad = reduce_pair(up_part, down_part)
        for m in samples:
            own = kept[m]
            inputs = [own["grad"], own["middle"], *own["n2"], second_gain, *own["att"]]
            inputs += [attend_scale, out_bias, own["q"], own["k"], own["v"], own["probs"]]
            outs = run(
                functools.partial(attend_backward, layer),
                inputs + attend_weights,
                [whole(v) for v in inputs] + [ANYWHERE] * 8,
                [state, act, head, head, head, act, ((4, width), F32), ((2, features), F32)],
                attend_scratch
                + [pltpu.VMEM((tokens, features), BF16), pltpu.SemaphoreType.DMA((8,))],
                "attend_backward",
                2 * attend_flops,
            )
            own.update(zip(("grad_middle", "grad_att", "gq", "gk", "gv"), outs))
            n1 = (outs[5], swap_x(outs[5]))
            carry[m] = (own["grad_middle"], own["current"], *n1)
            attend_sums.append(outs[6:])
        normed = [kept[m]["normed"] for m in samples]
        grad_att = [kept[m]["grad_att"] for m in samples]

        def attend_pairs(offset):
            return [
                (normed, spans("gq", heads_half, offset)),
                (normed, spans("gk", heads_half, offset)),
                (normed, spans("gv", heads_half, offset)),
                (grad_att, spans("mixed", heads_half, offset)),
            ]

        given = weight_grads(attend_pairs(heads_half), places_attend, None, 1, "attend_grads_given")
        taken = [swap_core(value) for value in given]
        part = weight_grads(attend_pairs(0), places_attend, taken, 1, "attend_grads")
        one, two = reduce_pair(
            jnp.concatenate(part[:2], axis=1), jnp.concatenate(part[2:], axis=1)
        )
        q_grad, k_grad = one[:, :heads_half], one[:, heads_half:]
        v_grad, o_grad = two[:, :heads_half], two[:, heads_half:]
        grads[layer] = (q_grad, k_grad, v_grad, o_grad, up_grad, down_grad)
        smalls[layer] = (
            sum(s[0] for s in feed_sums),
            sum(s[1] for s in feed_sums),
            sum(s[0] for s in attend_sums),
            sum(s[1] for s in attend_sums),
        )

    inputs_grad = []
    final_sums = []
    for m in samples:
        inputs = [*carry[m], first_gain]
        outs = run(
            finish_backward,
            inputs,
            [whole(v) for v in inputs],
            [state, ((2, width), F32)],
            [],
            "finish_backward",
            tokens * width,
        )
        inputs_grad.append(outs[0])
        final_sums.append(outs[1])
    final_sums = sum(final_sums)

    common = []
    narrow_own, narrow_other = [], []
    for layer in range(layers):
        feed_rows, feed_wide, attend_rows, attend_wide = smalls[layer]
        first_rows = final_sums if layer == 0 else smalls[layer - 1][0][2:4]
        common += [first_rows, attend_rows, feed_rows[0:2]]
        for target, start in ((narrow_own, 0), (narrow_other, 1)):
            a, b = start * heads_half, start * hidden_half
            target += [
                feed_wide[:, b : b + hidden_half].reshape(-1),
                attend_wide[:, a : a + heads_half].reshape(-1),
            ]
    common = jnp.concatenate(common, axis=0)
    common_count = common.shape[0]
    sent = jnp.concatenate([common.reshape(-1), *narrow_other])
    held = jnp.concatenate([common.reshape(-1), *narrow_own])
    total = held + swap_core(sent)
    split = common_count * width
    pieces = [total[:split].reshape(common_count, n, width // n).transpose(1, 0, 2).reshape(n, -1)]
    at = split
    lengths = []
    for layer in range(layers):
        for length in (hidden_half, heads_half, heads_half):
            pieces.append(total[at : at + length].reshape(n, length // n))
            lengths.append(length // n)
            at += length
    packed = jnp.concatenate(pieces, axis=1)
    if ring:
        mine = small_scatter(packed, n)
    else:
        mine = lax.psum_scatter(packed, "dp", scatter_dimension=0, tiled=True).reshape(-1)
    each = width // n
    vectors = mine[: common_count * each].reshape(layers, 8, each)
    at = common_count * each
    narrow = []
    for length in lengths:
        narrow.append(mine[at : at + length])
        at += length
    up_bias_grad = jnp.stack([narrow[3 * layer] for layer in range(layers)])
    query_bias_grad = jnp.stack([narrow[3 * layer + 1] for layer in range(layers)])
    value_bias_grad = jnp.stack([narrow[3 * layer + 2] for layer in range(layers)])

    def join(values):
        mine_now = jnp.stack([v.reshape(slots, width) for v in values])
        theirs = jnp.stack([swap_core(v).reshape(slots, width) for v in values])
        low = core == 0
        return jnp.concatenate(
            [jnp.where(low, mine_now, theirs), jnp.where(low, theirs, mine_now)], axis=0
        )

    stacked = [jnp.stack([grads[layer][i] for layer in range(layers)]) for i in range(6)]
    return (
        join(results),
        join(inputs_grad),
        vectors[:, 0],
        vectors[:, 1],
        stacked[0],
        stacked[1],
        stacked[2],
        query_bias_grad,
        value_bias_grad,
        stacked[3],
        vectors[:, 2],
        vectors[:, 3],
        vectors[:, 4],
        vectors[:, 5],
        stacked[4],
        up_bias_grad,
        stacked[5],
        vectors[:, 6],
        vectors[:, 7],
    )


def solution(mesh):
    return jax.shard_map(
        functools.partial(per_device, mesh.shape["dp"]),
        mesh=mesh,
        in_specs=(
            P("dp", None, None),
            P("dp", None),
            P(),
            P(),
            P(None, None, "mp"),
            P(None, None, "mp"),
            P(None, None, "mp"),
            P(None, "mp"),
            P(None, "mp"),
            P(None, None, "mp"),
            P(),
            P(),
            P(),
            P(),
            P(None, None, "mp"),
            P(None, "mp"),
            P(None, None, "mp"),
            P(),
            P(),
            P("dp", None, None),
        ),
        out_specs=(
            P("dp", None, None),
            P("dp", None, None),
            P(None, "dp"),
            P(None, "dp"),
            P(None, "dp", "mp"),
            P(None, "dp", "mp"),
            P(None, "dp", "mp"),
            P(None, ("mp", "dp")),
            P(None, ("mp", "dp")),
            P(None, "dp", "mp"),
            P(None, "dp"),
            P(None, "dp"),
            P(None, "dp"),
            P(None, "dp"),
            P(None, "dp", "mp"),
            P(None, ("mp", "dp")),
            P(None, "dp", "mp"),
            P(None, "dp"),
            P(None, "dp"),
        ),
        check_vma=False,
    )
```

time: 1930 us -> 527 us (0.27)
  waiting for transfers between devices: 1590 us -> 154 us
  Pallas kernels: 0 us -> 210 us
  matrix products: 139 us -> 0 us
  starting transfers between devices: 2.55 us -> 96.7 us
  other arithmetic: 88.3 us -> 27 us
  local copies, waits for them, and re-layouts: 83.1 us -> 27.4 us
    unnamed x35 -> x0, waiting for transfers between devices: 632 us -> none
    reduce_scatter x6 -> x0, waiting for transfers between devices: 587 us -> none  [the longest x1 153 us: per_device(): lax.psum_scatter(stacked[14], 'dp', scatter_dimension=1, tiled=True)]
    psum x7 -> x0, waiting for transfers between devices: 368 us -> none  [the longest x2 119 us: forward_layer(): fed = lax.psum(partial_feed.astype(jnp.bfloat16), 'mp').astype(jnp.float32)]
    pallas_call x0 -> x28, Pallas kernels: none -> 210 us  [the longest x20 152 us: run(): pl.pallas_call(body, out_shape=shapes, grid=(1,), in_specs=specs, out_spe...]
    ppermute x0 -> x103, waiting for transfers between devices: none -> 154 us  [the longest x28 77.9 us: ring_scatter(): two = lax.ppermute(two, 'dp', backward)]
    dot_general x46 -> x0, matrix products: 129 us -> none  [the longest x2 25.1 us: feed_pieces(): jnp.dot(normed2, weights_now[12], preferred_element_type=jnp.float32)]
    ppermute x0 -> x103, starting transfers between devices: none -> 96.7 us  [the longest x28 48.6 us: ring_scatter(): one = lax.ppermute(one, 'dp', forward)]
    reduce_sum x20 -> x0, other arithmetic: 61.3 us -> none  [the longest x8 31.8 us: norm_rows(): return center * lax.rsqrt(spread + EPSILON) * gain + shift]
  transfers between devices with their start and end apart: 24 -> 103, of which waited for: 24 -> 50; matrix products, arithmetic and copies ran while one was open for 5% -> 8% of each run, Pallas kernels for 0% -> 41%
where the time goes in v1:
time: 527 us; the launch traced here: 518 us
  Pallas kernels  210 us (40%)
  waiting for transfers between devices  154 us (29%)
  starting transfers between devices  96.7 us (18%)
  local copies, waits for them, and re-layouts  27.4 us (5%)
  other arithmetic  27 us (5%)
    pallas_call x20, Pallas kernels, run(): pl.pallas_call(body, out_shape=shapes, grid=(1,), in_specs=specs, out_spe...  152 us
    ppermute x28, waiting for transfers between devices, ring_scatter(): two = lax.ppermute(two, 'dp', backward)  77.9 us
    pallas_call x8, Pallas kernels, weight_grads(): pl.pallas_call(functools.partial(weight_grad, places.shape[1], count, oth...  58.5 us
    ppermute x28, waiting for transfers between devices, ring_scatter(): one = lax.ppermute(one, 'dp', forward)  51.8 us
    ppermute x28, starting transfers between devices, ring_scatter(): one = lax.ppermute(one, 'dp', forward)  48.6 us
    ppermute x16, starting transfers between devices, swap_x(): return lax.ppermute(value, 'mp', [(i, i ^ 2) for i in range(4)])  19.6 us
    ppermute x24, waiting for transfers between devices, swap_core(): return lax.ppermute(value, 'mp', [(i, i ^ 1) for i in range(4)])  14.9 us
    unnamed x135, local copies, waits for them, and re-layouts  14.6 us
  transfers between devices with their start and end apart: 103, of which 50 were waited for; matrix products, arithmetic and copies ran while one was open for 8% of the time, Pallas kernels for 41%

profile of v1, /device:TPU:0, one launch (start us, length us, event | category | flops | bytes accessed | tf_op | source)
XLA Modules:
  0.0 517.7 jit_solution(4482947822293033483)
XLA Ops:
  3.0 6.0 %collective-permute-done = f32[2,1536]{1,0:T(2,128)S(1)} collective-permute-done((f32[2,1536]{1,0:T(2,128)S(1)}, f32[2,1536]{1,0:T(2,128)S(1)}, u32[]{:S(2)}, u32[]{:S(2)}) %collective-permute-start) | collective-permute-done | bytes 12320 | tf_op jit(solution)/shard_map/ppermute | solution.py:479
  14.0 3.3 collective-permute-done.2.refs_9_.refs_13_.refs_16_
  20.4 7.0 %attend_forward.6 = (f32[256,1024]{1,0:T(8,128)}, bf16[256,1024]{1,0:T(8,128)(2,1)}, bf16[256,512]{1,0:T(8,128)(2,1)}, bf16[256,512]{1,0:T(8,128)(2,1)}, bf16[25...) custom-call(bf16[2,256,1024]{2,1,0:T(8,128)(2,1)} %constant_dynamic-slic, ...), custom_call_target="tpu_custom_call" | custom-call | flops 1342177280 | bytes 9187328 | tf_op jit(solution)/shard_map/attend_forward/pallas_call | solution.py:346
  27.4 2.9 collective-permute-start.11
  30.4 7.0 %attend_forward.4 = (f32[256,1024]{1,0:T(8,128)}, bf16[256,1024]{1,0:T(8,128)(2,1)}, bf16[256,512]{1,0:T(8,128)(2,1)}, bf16[256,512]{1,0:T(8,128)(2,1)}, bf16[25...) custom-call(bf16[2,256,1024]{2,1,0:T(8,128)(2,1)} %constant_dynamic-slic, ...), custom_call_target="tpu_custom_call" | custom-call | flops 1342177280 | bytes 9187328 | tf_op jit(solution)/shard_map/attend_forward/pallas_call | solution.py:346
  38.1 5.2 collective-permute-done.11.refs_2_.refs_6_
  44.0 9.0 %feed_forward.6 = (f32[256,1024]{1,0:T(8,128)}, bf16[256,1024]{1,0:T(8,128)(2,1)}, bf16[256,1024]{1,0:T(8,128)(2,1)}, bf16[256,1024]{1,0:T(8,128)(2,1)}, bf16[25...) custom-call(f32[256,1024]{1,0:T(8,128)} %get-tuple-element.175.refs_0_.deep, ...), custom_call_target="tpu_custom_call" | custom-call | flops 2147483648 | bytes 12615680 | tf_op jit(solution)/shard_map/feed_forward/pallas_call | solution.py:346
  56.0 9.5 %feed_forward.4 = (f32[256,1024]{1,0:T(8,128)}, bf16[256,1024]{1,0:T(8,128)(2,1)}, bf16[256,1024]{1,0:T(8,128)(2,1)}, bf16[256,1024]{1,0:T(8,128)(2,1)}, bf16[25...) custom-call(f32[256,1024]{1,0:T(8,128)} %get-tuple-element.167.refs_0_.deep, ...), custom_call_target="tpu_custom_call" | custom-call | flops 2147483648 | bytes 12615680 | tf_op jit(solution)/shard_map/feed_forward/pallas_call | solution.py:346
  67.1 7.5 %attend_forward.7 = (f32[256,1024]{1,0:T(8,128)}, bf16[256,1024]{1,0:T(8,128)(2,1)}, bf16[256,512]{1,0:T(8,128)(2,1)}, bf16[256,512]{1,0:T(8,128)(2,1)}, bf16[25...) custom-call(f32[256,1024]{1,0:T(8,128)} %get-tuple-element.177.refs_0_.r, ...), custom_call_target="tpu_custom_call" | custom-call | flops 1342177280 | bytes 8679424 | tf_op jit(solution)/shard_map/attend_forward/pallas_call | solution.py:346
  76.2 3.4 collective-permute-done.8.refs_2_.refs_6_
  80.4 7.5 %attend_forward.5 = (f32[256,1024]{1,0:T(8,128)}, bf16[256,1024]{1,0:T(8,128)(2,1)}, bf16[256,512]{1,0:T(8,128)(2,1)}, bf16[256,512]{1,0:T(8,128)(2,1)}, bf16[25...) custom-call(f32[256,1024]{1,0:T(8,128)} %get-tuple-element.169.refs_0_.r, ...), custom_call_target="tpu_custom_call" | custom-call | flops 1342177280 | bytes 8679424 | tf_op jit(solution)/shard_map/attend_forward/pallas_call | solution.py:346
  91.7 9.1 %feed_forward.7 = (f32[256,1024]{1,0:T(8,128)}, bf16[256,1024]{1,0:T(8,128)(2,1)}, bf16[256,1024]{1,0:T(8,128)(2,1)}, bf16[256,1024]{1,0:T(8,128)(2,1)}, bf16[25...) custom-call(f32[256,1024]{1,0:T(8,128)} %get-tuple-element.179.refs_0_.refs_1_, ...), custom_call_target="tpu_custom_call" | custom-call | flops 2147483648 | bytes 12615680 | tf_op jit(solution)/shard_map/feed_forward/pallas_call | solution.py:346
  103.1 9.3 %feed_forward.5 = (f32[256,1024]{1,0:T(8,128)}, bf16[256,1024]{1,0:T(8,128)(2,1)}, bf16[256,1024]{1,0:T(8,128)(2,1)}, bf16[256,1024]{1,0:T(8,128)(2,1)}, bf16[25...) custom-call(f32[256,1024]{1,0:T(8,128)} %get-tuple-element.171.refs_0_.refs_1_, ...), custom_call_target="tpu_custom_call" | custom-call | flops 2147483648 | bytes 12615680 | tf_op jit(solution)/shard_map/feed_forward/pallas_call | solution.py:346
  115.0 2.6 finish_forward.3
  117.6 8.4 %feed_backward.6 = (f32[256,1024]{1,0:T(8,128)}, bf16[256,1024]{1,0:T(8,128)(2,1)}, bf16[256,1024]{1,0:T(8,128)(2,1)}, bf16[256,1024]{1,0:T(8,128)(2,1)}, bf16[2...) custom-call(bf16[2,256,1024]{2,1,0:T(8,128)(2,1)} %constant_dynamic-slice_fusion.refs_0_, ...), custom_call_target="tpu_custom_call" | custom-call | flops 2147483648 | bytes 12099584 | tf_op jit(solution)/shard_map/feed_backward/pallas_call | solution.py:346
  128.3 8.5 %feed_backward.4 = (f32[256,1024]{1,0:T(8,128)}, bf16[256,1024]{1,0:T(8,128)(2,1)}, bf16[256,1024]{1,0:T(8,128)(2,1)}, bf16[256,1024]{1,0:T(8,128)(2,1)}, bf16[2...) custom-call(bf16[2,256,1024]{2,1,0:T(8,128)(2,1)} %constant_dynamic-slice_fusion.refs_0_, ...), custom_call_target="tpu_custom_call" | custom-call | flops 2147483648 | bytes 12099584 | tf_op jit(solution)/shard_map/feed_backward/pallas_call | solution.py:346
  138.2 2.6 finish_forward.2
  140.8 8.2 %feed_grads_given.3 = (bf16[1024,1024]{1,0:T(8,128)(2,1)}, bf16[1024,1024]{1,0:T(8,128)(2,1)}) custom-call(s32[2,8]{1,0:T(2,128)} %pad_add_fusion.1.places, bf16[256,1024]{1,0:T(8,128)(2,1)} %get-tuple-element.298.refs_0_, bf16[256,1024]{1,0:T(8,128)(2,1)} %get-tuple-element.299.refs_1_, bf16[256,1024]{1,0:T(8,128)(2,1)} %get-tuple-element.300.refs_2_, ...), custom_call_target="tpu_custom_call" | custom-call | flops 2147483648 | bytes 8388608 | tf_op jit(solution)/shard_map/feed_grads_given/pallas_call | solution.py:389
  149.8 9.4 %attend_backward.6 = (f32[256,1024]{1,0:T(8,128)}, bf16[256,1024]{1,0:T(8,128)(2,1)}, bf16[256,512]{1,0:T(8,128)(2,1)}, bf16[256,512]{1,0:T(8,128)(2,1)}, bf16[2...) custom-call(f32[256,1024]{1,0:T(8,128)} %get-tuple-element.206.refs_0_, ...), custom_call_target="tpu_custom_call" | custom-call | flops 2684354560 | bytes 7261184 | tf_op jit(solution)/shard_map/attend_backward/pallas_call | solution.py:346
  161.6 9.4 %attend_backward.4 = (f32[256,1024]{1,0:T(8,128)}, bf16[256,1024]{1,0:T(8,128)(2,1)}, bf16[256,512]{1,0:T(8,128)(2,1)}, bf16[256,512]{1,0:T(8,128)(2,1)}, bf16[2...) custom-call(f32[256,1024]{1,0:T(8,128)} %get-tuple-element.185.refs_0_, ...), custom_call_target="tpu_custom_call" | custom-call | flops 2684354560 | bytes 7261184 | tf_op jit(solution)/shard_map/attend_backward/pallas_call | solution.py:346
  172.3 5.9 %attend_grads_given.3 = (bf16[1024,256]{1,0:T(8,128)(2,1)}, bf16[1024,256]{1,0:T(8,128)(2,1)}, bf16[1024,256]{1,0:T(8,128)(2,1)}, bf16[1024,256]{1,0:T(8,128)(2,1)}) custom-call(s32[4,8]{1,0:T(4,128)} %pad_add_fusion.places, bf16[256,1024]{1,0:T(8,128)(2,1)} %get-tuple-element.261.refs_0_.refs_2_.refs_4_, ...), custom_call_target="tpu_custom_call" | custom-call | flops 1073741824 | bytes 8388608 | tf_op jit(solution)/shard_map/attend_grads_given/pallas_call | solution.py:389
  181.5 9.6 %feed_backward.7 = (f32[256,1024]{1,0:T(8,128)}, bf16[256,1024]{1,0:T(8,128)(2,1)}, bf16[256,1024]{1,0:T(8,128)(2,1)}, bf16[256,1024]{1,0:T(8,128)(2,1)}, bf16[2...) custom-call(f32[256,1024]{1,0:T(8,128)} %get-tuple-element.212.refs_0_, ...), custom_call_target="tpu_custom_call" | custom-call | flops 2147483648 | bytes 11591680 | tf_op jit(solution)/shard_map/feed_backward/pallas_call | solution.py:346
  191.9 9.2 %feed_backward.5 = (f32[256,1024]{1,0:T(8,128)}, bf16[256,1024]{1,0:T(8,128)(2,1)}, bf16[256,1024]{1,0:T(8,128)(2,1)}, bf16[256,1024]{1,0:T(8,128)(2,1)}, bf16[2...) custom-call(f32[256,1024]{1,0:T(8,128)} %get-tuple-element.191.refs_0_, ...), custom_call_target="tpu_custom_call" | custom-call | flops 2147483648 | bytes 11591680 | tf_op jit(solution)/shard_map/feed_backward/pallas_call | solution.py:346
  205.6 6.4 %attend_grads.3 = (bf16[1024,256]{1,0:T(8,128)(2,1)}, bf16[1024,256]{1,0:T(8,128)(2,1)}, bf16[1024,256]{1,0:T(8,128)(2,1)}, bf16[1024,256]{1,0:T(8,128)(2,1)}) custom-call(s32[4,8]{1,0:T(4,128)} %pad_add_fusion.places, bf16[256,1024]{1,0:T(8,128)(2,1)} %get-tuple-element.261.refs_0_.refs_2_.refs_4_, ...), custom_call_target="tpu_custom_call" | custom-call | flops 1073741824 | bytes 10485760 | tf_op jit(solution)/shard_map/attend_grads/pallas_call | solution.py:389
  216.1 7.9 %feed_grads_given.2 = (bf16[1024,1024]{1,0:T(8,128)(2,1)}, bf16[1024,1024]{1,0:T(8,128)(2,1)}) custom-call(s32[2,8]{1,0:T(2,128)} %pad_add_fusion.1.places, bf16[256,1024]{1,0:T(8,128)(2,1)} %get-tuple-element.283.refs_0_, bf16[256,1024]{1,0:T(8,128)(2,1)} %get-tuple-element.284.refs_1_, bf16[256,1024]{1,0:T(8,128)(2,1)} %get-tuple-element.285.refs_2_, ...), custom_call_target="tpu_custom_call" | custom-call | flops 2147483648 | bytes 8388608 | tf_op jit(solution)/shard_map/feed_grads_given/pallas_call | solution.py:389
  224.6 4.5 collective-permute-done.64
  230.7 3.3 collective-permute-done.51
  234.5 4.5 collective-permute-done.65
  240.6 3.3 collective-permute-done.52
  244.5 5.7 %collective-permute-done.66 = bf16[128,512]{1,0:T(8,128)(2,1)S(1)} collective-permute-done((bf16[128,512]{1,0:T(8,128)(2,1)S(1)}, bf16[128,512]{1,0:T(8,128)(2,1)S(1)}, u32[]{:S(2)}, u32[]{:S(2)}) %collective-permute-start.66) | collective-permute-done | bytes 131104 | tf_op jit(solution)/shard_map/ppermute | solution.py:421
  252.6 9.4 %attend_backward.7 = (f32[256,1024]{1,0:T(8,128)}, bf16[256,1024]{1,0:T(8,128)(2,1)}, bf16[256,512]{1,0:T(8,128)(2,1)}, bf16[256,512]{1,0:T(8,128)(2,1)}, bf16[2...) custom-call(f32[256,1024]{1,0:T(8,128)} %get-tuple-element.216.refs_0_, ...), custom_call_target="tpu_custom_call" | custom-call | flops 2684354560 | bytes 7261184 | tf_op jit(solution)/shard_map/attend_backward/pallas_call | solution.py:346
  263.4 9.4 %attend_backward.5 = (f32[256,1024]{1,0:T(8,128)}, bf16[256,1024]{1,0:T(8,128)(2,1)}, bf16[256,512]{1,0:T(8,128)(2,1)}, bf16[256,512]{1,0:T(8,128)(2,1)}, bf16[2...) custom-call(f32[256,1024]{1,0:T(8,128)} %get-tuple-element.195.refs_0_, ...), custom_call_target="tpu_custom_call" | custom-call | flops 2684354560 | bytes 7261184 | tf_op jit(solution)/shard_map/attend_backward/pallas_call | solution.py:346
  276.8 5.5 %attend_grads_given.2 = (bf16[1024,256]{1,0:T(8,128)(2,1)}, bf16[1024,256]{1,0:T(8,128)(2,1)}, bf16[1024,256]{1,0:T(8,128)(2,1)}, bf16[1024,256]{1,0:T(8,128)(2,1)}) custom-call(s32[4,8]{1,0:T(4,128)} %pad_add_fusion.places, bf16[256,1024]{1,0:T(8,128)(2,1)} %get-tuple-element.243.refs_0_.refs_2_.refs_4_, ...), custom_call_target="tpu_custom_call" | custom-call | flops 1073741824 | bytes 8388608 | tf_op jit(solution)/shard_map/attend_grads_given/pallas_call | solution.py:389
  282.9 5.2 %collective-permute-done.68 = bf16[128,512]{1,0:T(8,128)(2,1)S(1)} collective-permute-done((bf16[128,512]{1,0:T(8,128)(2,1)S(1)}, bf16[128,512]{1,0:T(8,128)(2,1)S(1)}, u32[]{:S(2)}, u32[]{:S(2)}) %collective-permute-start.68) | collective-permute-done | bytes 131104 | tf_op jit(solution)/shard_map/ppermute | solution.py:421
  289.7 3.4 collective-permute-done.55
  293.6 4.5 collective-permute-done.69
  299.6 3.4 collective-permute-done.56
  303.7 4.5 collective-permute-done.70
  309.9 3.6 finish_backward.3
  314.3 3.6 finish_backward.2
  321.8 6.5 %attend_grads.2 = (bf16[1024,256]{1,0:T(8,128)(2,1)}, bf16[1024,256]{1,0:T(8,128)(2,1)}, bf16[1024,256]{1,0:T(8,128)(2,1)}, bf16[1024,256]{1,0:T(8,128)(2,1)}) custom-call(s32[4,8]{1,0:T(4,128)} %pad_add_fusion.places, bf16[256,1024]{1,0:T(8,128)(2,1)} %get-tuple-element.243.refs_0_.refs_2_.refs_4_, ...), custom_call_target="tpu_custom_call" | custom-call | flops 1073741824 | bytes 10485760 | tf_op jit(solution)/shard_map/attend_grads/pallas_call | solution.py:389
  330.5 9.0 %feed_grads.3 = (bf16[1024,1024]{1,0:T(8,128)(2,1)}, bf16[1024,1024]{1,0:T(8,128)(2,1)}) custom-call(s32[2,8]{1,0:T(2,128)} %pad_add_fusion.1.places, bf16[256,1024]{1,0:T(8,128)(2,1)} %get-tuple-element.298.refs_0_, bf16[256,1024]{1,0:T(8,128)(2,1)} %get-tuple-element.299.refs_1_, bf16[256,1024]{1,0:T(8,128)(2,1)} %get-tuple-element.300.refs_2_, ...), custom_call_target="tpu_custom_call" | custom-call | flops 2147483648 | bytes 12582912 | tf_op jit(solution)/shard_map/feed_grads/pallas_call | solution.py:389
  343.0 4.3 collective-permute-start.34
  366.3 3.5 collective-permute-done.40
  370.4 4.3 collective-permute-done.58
  377.4 5.0 collective-permute-done.82
  384.1 3.6 collective-permute-done.59
  390.0 2.6 collective-permute-done.42
  393.0 5.0 collective-permute-done.60
  406.8 2.5 collective-permute-done.61
  420.6 4.9 collective-permute-done.62
  427.6 2.9 collective-permute-done.45
  432.1 4.8 collective-permute-done.63
  440.5 9.0 %feed_grads.2 = (bf16[1024,1024]{1,0:T(8,128)(2,1)}, bf16[1024,1024]{1,0:T(8,128)(2,1)}) custom-call(s32[2,8]{1,0:T(2,128)} %pad_add_fusion.1.places, bf16[256,1024]{1,0:T(8,128)(2,1)} %get-tuple-element.283.refs_0_, bf16[256,1024]{1,0:T(8,128)(2,1)} %get-tuple-element.284.refs_1_, bf16[256,1024]{1,0:T(8,128)(2,1)} %get-tuple-element.285.refs_2_, ...), custom_call_target="tpu_custom_call" | custom-call | flops 2147483648 | bytes 12582912 | tf_op jit(solution)/shard_map/feed_grads/pallas_call | solution.py:389
  453.9 2.4 fusion.1
  456.3 2.5 pad_maximum_fusion
  463.4 4.8 collective-permute-done.100
  468.4 5.3 %collective-permute-done.90 = bf16[128,1024]{1,0:T(8,128)(2,1)S(1)} collective-permute-done((bf16[128,1024]{1,0:T(8,128)(2,1)S(1)}, bf16[128,1024]{1,0:T(8,128)(2,1)S(1)}, u32[]{:S(2)}, u32[]{:S(2)}) %collective-permute-start.90) | collective-permute-done | bytes 262176 | tf_op jit(solution)/shard_map/ppermute | solution.py:421
  477.8 5.2 collective-permute-done.91
  483.7 2.7 collective-permute-done.75
  495.7 3.2 collective-permute-done.93
  499.5 3.6 collective-permute-done.77
  506.4 3.2 collective-permute-done.78
  513.3 2.8 collective-permute-done.79
  (436 shorter events, 162.5 us)
Async XLA Ops:
  0.7 42.6 %collective-permute-start.6 = (bf16[2,1024,1024]{2,1,0:T(8,128)(2,1)}, bf16[2,1024,1024]{2,1,0:T(8,128)(2,1)}, u32[]{:S(2)}, u32[]{:S(2)}) collective-permute-start(bf16[2,1024,1024]{2,1,0:T(8,128)(2,1)} %refs_11_.3), channel_id=1, source_target_pairs={{0,1},{1,0},{2,3},{3,2},{4,5},{5,4},{6,7},{7,6},{8,9},{9,8},{10,11... | collective-permute-start | bytes 12582920 | tf_op jit(solution)/shard_map/ppermute | solution.py:479
  1.2 42.1 %collective-permute-start.7 = (bf16[2,1024,1024]{2,1,0:T(8,128)(2,1)}, bf16[2,1024,1024]{2,1,0:T(8,128)(2,1)}, u32[]{:S(2)}, u32[]{:S(2)}) collective-permute-start(bf16[2,1024,1024]{2,1,0:T(8,128)(2,1)} %refs_13_.10), channel_id=1, source_target_pairs={{0,1},{1,0},{2,3},{3,2},{4,5},{5,4},{6,7},{7,6},{8,9},{9,8},{10,11... | collective-permute-start | bytes 12582920 | tf_op jit(solution)/shard_map/ppermute | solution.py:479
  1.3 9.2 %collective-permute-start.1 = (bf16[2,1024,256]{2,1,0:T(8,128)(2,1)}, bf16[2,1024,256]{2,1,0:T(8,128)(2,1)S(1)}, u32[]{:S(2)}, u32[]{:S(2)}) collective-permute-start(bf16[2,1024,256]{2,1,0:T(8,128)(2,1)} %refs_13_.11), channel_id=1, source_target_pairs={{0,1},{1,0},{2,3},{3,2},{4,5},{5,4},{6,7},{7,6},{8,9},{9,8},{10,11... | collective-permute-start | bytes 3145736 | tf_op jit(solution)/shard_map/ppermute | solution.py:479
  2.5 14.8 %collective-permute-start.2 = (bf16[2,1024,256]{2,1,0:T(8,128)(2,1)}, bf16[2,1024,256]{2,1,0:T(8,128)(2,1)}, u32[]{:S(2)}, u32[]{:S(2)}) collective-permute-start(bf16[2,1024,256]{2,1,0:T(8,128)(2,1)} %refs_15_.7), channel_id=1, source_target_pairs={{0,1},{1,0},{2,3},{3,2},{4,5},{5,4},{6,7},{7,6},{8,9},{9,8},{10,11... | collective-permute-start | bytes 3145736 | tf_op jit(solution)/shard_map/ppermute | solution.py:479
  8.9 9.9 %collective-permute-start.3 = (bf16[2,1024,256]{2,1,0:T(8,128)(2,1)}, bf16[2,1024,256]{2,1,0:T(8,128)(2,1)}, u32[]{:S(2)}, u32[]{:S(2)}) collective-permute-start(bf16[2,1024,256]{2,1,0:T(8,128)(2,1)} %refs_17_.7), channel_id=1, source_target_pairs={{0,1},{1,0},{2,3},{3,2},{4,5},{5,4},{6,7},{7,6},{8,9},{9,8},{10,11... | collective-permute-start | bytes 3145736 | tf_op jit(solution)/shard_map/ppermute | solution.py:479
  10.5 9.9 %collective-permute-start.4 = (bf16[2,1024,256]{2,1,0:T(8,128)(2,1)}, bf16[2,1024,256]{2,1,0:T(8,128)(2,1)}, u32[]{:S(2)}, u32[]{:S(2)}) collective-permute-start(bf16[2,1024,256]{2,1,0:T(8,128)(2,1)} %refs_19_.7), channel_id=1, source_target_pairs={{0,1},{1,0},{2,3},{3,2},{4,5},{5,4},{6,7},{7,6},{8,9},{9,8},{10,11... | collective-permute-start | bytes 3145736 | tf_op jit(solution)/shard_map/ppermute | solution.py:479
  27.4 15.8 %collective-permute-start.11 = (bf16[256,1024]{1,0:T(8,128)(2,1)}, bf16[256,1024]{1,0:T(8,128)(2,1)S(1)}, u32[]{:S(2)}, u32[]{:S(2)}) collective-permute-start(bf16[256,1024]{1,0:T(8,128)(2,1)} %get-tuple-element.176.refs_1_.refs_5_), channel_id=1, source_target_pairs={{0,2},{1,3},{2,0},{3,1},{4,6},{5,7},{6,4},{7,5},{8,10},{9,11},{10,... | collective-permute-start | bytes 1572872 | tf_op jit(solution)/shard_map/ppermute | solution.py:482
  37.4 17.8 %collective-permute-start.5 = (bf16[256,1024]{1,0:T(8,128)(2,1)}, bf16[256,1024]{1,0:T(8,128)(2,1)S(1)}, u32[]{:S(2)}, u32[]{:S(2)}) collective-permute-start(bf16[256,1024]{1,0:T(8,128)(2,1)} %get-tuple-element.168.refs_1_.refs_5_), channel_id=1, source_target_pairs={{0,2},{1,3},{2,0},{3,1},{4,6},{5,7},{6,4},{7,5},{8,10},{9,11},{10,... | collective-permute-start | bytes 1572872 | tf_op jit(solution)/shard_map/ppermute | solution.py:482
  53.1 13.2 %collective-permute-start.12 = (bf16[256,1024]{1,0:T(8,128)(2,1)}, bf16[256,1024]{1,0:T(8,128)(2,1)S(1)}, u32[]{:S(2)}, u32[]{:S(2)}) collective-permute-start(bf16[256,1024]{1,0:T(8,128)(2,1)} %get-tuple-element.178.refs_1_.refs_5_), channel_id=1, source_target_pairs={{0,2},{1,3},{2,0},{3,1},{4,6},{5,7},{6,4},{7,5},{8,10},{9,11},{10,... | collective-permute-start | bytes 1572872 | tf_op jit(solution)/shard_map/ppermute | solution.py:482
  65.6 14.1 %collective-permute-start.8 = (bf16[256,1024]{1,0:T(8,128)(2,1)}, bf16[256,1024]{1,0:T(8,128)(2,1)S(1)}, u32[]{:S(2)}, u32[]{:S(2)}) collective-permute-start(bf16[256,1024]{1,0:T(8,128)(2,1)} %get-tuple-element.170.refs_1_.refs_5_), channel_id=1, source_target_pairs={{0,2},{1,3},{2,0},{3,1},{4,6},{5,7},{6,4},{7,5},{8,10},{9,11},{10,... | collective-permute-start | bytes 1572872 | tf_op jit(solution)/shard_map/ppermute | solution.py:482
  74.7 16.2 %collective-permute-start.13 = (bf16[256,1024]{1,0:T(8,128)(2,1)}, bf16[256,1024]{1,0:T(8,128)(2,1)S(1)}, u32[]{:S(2)}, u32[]{:S(2)}) collective-permute-start(bf16[256,1024]{1,0:T(8,128)(2,1)} %get-tuple-element.180.refs_1_.refs_5_), channel_id=1, source_target_pairs={{0,2},{1,3},{2,0},{3,1},{4,6},{5,7},{6,4},{7,5},{8,10},{9,11},{10,... | collective-permute-start | bytes 1572872 | tf_op jit(solution)/shard_map/ppermute | solution.py:482
  88.0 14.4 %collective-permute-start.9 = (bf16[256,1024]{1,0:T(8,128)(2,1)}, bf16[256,1024]{1,0:T(8,128)(2,1)S(1)}, u32[]{:S(2)}, u32[]{:S(2)}) collective-permute-start(bf16[256,1024]{1,0:T(8,128)(2,1)} %get-tuple-element.172.refs_1_.refs_5_), channel_id=1, source_target_pairs={{0,2},{1,3},{2,0},{3,1},{4,6},{5,7},{6,4},{7,5},{8,10},{9,11},{10,... | collective-permute-start | bytes 1572872 | tf_op jit(solution)/shard_map/ppermute | solution.py:482
  100.8 13.4 %collective-permute-start.14 = (bf16[256,1024]{1,0:T(8,128)(2,1)}, bf16[256,1024]{1,0:T(8,128)(2,1)S(1)}, u32[]{:S(2)}, u32[]{:S(2)}) collective-permute-start(bf16[256,1024]{1,0:T(8,128)(2,1)} %get-tuple-element.182.mine.refs_1_), channel_id=1, source_target_pairs={{0,2},{1,3},{2,0},{3,1},{4,6},{5,7},{6,4},{7,5},{8,10},{9,11},{10,... | collective-permute-start | bytes 1572872 | tf_op jit(solution)/shard_map/ppermute | solution.py:482
  112.5 15.0 %collective-permute-start.10 = (bf16[256,1024]{1,0:T(8,128)(2,1)}, bf16[256,1024]{1,0:T(8,128)(2,1)S(1)}, u32[]{:S(2)}, u32[]{:S(2)}) collective-permute-start(bf16[256,1024]{1,0:T(8,128)(2,1)} %get-tuple-element.174.mine.refs_1_), channel_id=1, source_target_pairs={{0,2},{1,3},{2,0},{3,1},{4,6},{5,7},{6,4},{7,5},{8,10},{9,11},{10,... | collective-permute-start | bytes 1572872 | tf_op jit(solution)/shard_map/ppermute | solution.py:482
  117.6 60.7 %collective-permute-start.16 = (bf16[256,1024]{1,0:T(8,128)(2,1)}, bf16[256,1024]{1,0:T(8,128)(2,1)S(1)}, u32[]{:S(2)}, u32[]{:S(2)}) collective-permute-start(bf16[256,1024]{1,0:T(8,128)(2,1)} %finish_forward.3), channel_id=1, source_target_pairs={{0,1},{1,0},{2,3},{3,2},{4,5},{5,4},{6,7},{7,6},{8,9},{9,8},{10,11... | collective-permute-start | bytes 1572872 | tf_op jit(solution)/shard_map/ppermute | solution.py:479
  126.0 23.0 %collective-permute-start.21 = (bf16[256,1024]{1,0:T(8,128)(2,1)}, bf16[256,1024]{1,0:T(8,128)(2,1)S(1)}, u32[]{:S(2)}, u32[]{:S(2)}) collective-permute-start(bf16[256,1024]{1,0:T(8,128)(2,1)} %get-tuple-element.207.refs_2_), channel_id=1, source_target_pairs={{0,2},{1,3},{2,0},{3,1},{4,6},{5,7},{6,4},{7,5},{8,10},{9,11},{10,... | collective-permute-start | bytes 1572872 | tf_op jit(solution)/shard_map/ppermute | solution.py:482
  137.5 23.2 %collective-permute-start.17 = (bf16[256,1024]{1,0:T(8,128)(2,1)}, bf16[256,1024]{1,0:T(8,128)(2,1)S(1)}, u32[]{:S(2)}, u32[]{:S(2)}) collective-permute-start(bf16[256,1024]{1,0:T(8,128)(2,1)} %get-tuple-element.186.refs_2_), channel_id=1, source_target_pairs={{0,2},{1,3},{2,0},{3,1},{4,6},{5,7},{6,4},{7,5},{8,10},{9,11},{10,... | collective-permute-start | bytes 1572872 | tf_op jit(solution)/shard_map/ppermute | solution.py:482
  140.8 38.1 %collective-permute-start.15 = (bf16[256,1024]{1,0:T(8,128)(2,1)}, bf16[256,1024]{1,0:T(8,128)(2,1)S(1)}, u32[]{:S(2)}, u32[]{:S(2)}) collective-permute-start(bf16[256,1024]{1,0:T(8,128)(2,1)} %finish_forward.2), channel_id=1, source_target_pairs={{0,1},{1,0},{2,3},{3,2},{4,5},{5,4},{6,7},{7,6},{8,9},{9,8},{10,11... | collective-permute-start | bytes 1572872 | tf_op jit(solution)/shard_map/ppermute | solution.py:479
  159.3 21.4 %collective-permute-start.22 = (bf16[256,1024]{1,0:T(8,128)(2,1)}, bf16[256,1024]{1,0:T(8,128)(2,1)S(1)}, u32[]{:S(2)}, u32[]{:S(2)}) collective-permute-start(bf16[256,1024]{1,0:T(8,128)(2,1)} %get-tuple-element.213.refs_2_), channel_id=1, source_target_pairs={{0,2},{1,3},{2,0},{3,1},{4,6},{5,7},{6,4},{7,5},{8,10},{9,11},{10,... | collective-permute-start | bytes 1572872 | tf_op jit(solution)/shard_map/ppermute | solution.py:482
  171.7 19.4 %collective-permute-start.18 = (bf16[256,1024]{1,0:T(8,128)(2,1)}, bf16[256,1024]{1,0:T(8,128)(2,1)S(1)}, u32[]{:S(2)}, u32[]{:S(2)}) collective-permute-start(bf16[256,1024]{1,0:T(8,128)(2,1)} %get-tuple-element.192.refs_2_), channel_id=1, source_target_pairs={{0,2},{1,3},{2,0},{3,1},{4,6},{5,7},{6,4},{7,5},{8,10},{9,11},{10,... | collective-permute-start | bytes 1572872 | tf_op jit(solution)/shard_map/ppermute | solution.py:482
  178.2 23.7 %collective-permute-start.46 = (bf16[1024,256]{1,0:T(8,128)(2,1)}, bf16[1024,256]{1,0:T(8,128)(2,1)S(1)}, u32[]{:S(2)}, u32[]{:S(2)}) collective-permute-start(bf16[1024,256]{1,0:T(8,128)(2,1)} %get-tuple-element.273), channel_id=1, source_target_pairs={{0,1},{1,0},{2,3},{3,2},{4,5},{5,4},{6,7},{7,6},{8,9},{9,8},{10,11... | collective-permute-start | bytes 1572872 | tf_op jit(solution)/shard_map/ppermute | solution.py:479
  178.3 24.1 %collective-permute-start.47 = (bf16[1024,256]{1,0:T(8,128)(2,1)}, bf16[1024,256]{1,0:T(8,128)(2,1)S(1)}, u32[]{:S(2)}, u32[]{:S(2)}) collective-permute-start(bf16[1024,256]{1,0:T(8,128)(2,1)} %get-tuple-element.274), channel_id=1, source_target_pairs={{0,1},{1,0},{2,3},{3,2},{4,5},{5,4},{6,7},{7,6},{8,9},{9,8},{10,11... | collective-permute-start | bytes 1572872 | tf_op jit(solution)/shard_map/ppermute | solution.py:479
  178.8 25.1 %collective-permute-start.48 = (bf16[1024,256]{1,0:T(8,128)(2,1)}, bf16[1024,256]{1,0:T(8,128)(2,1)S(1)}, u32[]{:S(2)}, u32[]{:S(2)}) collective-permute-start(bf16[1024,256]{1,0:T(8,128)(2,1)} %get-tuple-element.275), channel_id=1, source_target_pairs={{0,1},{1,0},{2,3},{3,2},{4,5},{5,4},{6,7},{7,6},{8,9},{9,8},{10,11... | collective-permute-start | bytes 1572872 | tf_op jit(solution)/shard_map/ppermute | solution.py:479
  180.7 23.9 %collective-permute-start.49 = (bf16[1024,256]{1,0:T(8,128)(2,1)S(1)}, bf16[1024,256]{1,0:T(8,128)(2,1)S(1)}, u32[]{:S(2)}, u32[]{:S(2)}) collective-permute-start(bf16[1024,256]{1,0:T(8,128)(2,1)S(1)} %copy-done.56), channel_id=1, source_target_pairs={{0,1},{1,0},{2,3},{3,2},{4,5},{5,4},{6,7},{7,6},{8,9},{9,8},{10,11... | collective-permute-start | bytes 1572872 | tf_op jit(solution)/shard_map/ppermute | solution.py:479
  191.1 139.4 %collective-permute-start.80 = (bf16[1024,1024]{1,0:T(8,128)(2,1)}, bf16[1024,1024]{1,0:T(8,128)(2,1)}, u32[]{:S(2)}, u32[]{:S(2)}) collective-permute-start(bf16[1024,1024]{1,0:T(8,128)(2,1)} %get-tuple-element.310), channel_id=1, source_target_pairs={{0,1},{1,0},{2,3},{3,2},{4,5},{5,4},{6,7},{7,6},{8,9},{9,8},{10,11... | collective-permute-start | bytes 6291464 | tf_op jit(solution)/shard_map/ppermute | solution.py:479
  201.9 128.5 %collective-permute-start.81 = (bf16[1024,1024]{1,0:T(8,128)(2,1)}, bf16[1024,1024]{1,0:T(8,128)(2,1)}, u32[]{:S(2)}, u32[]{:S(2)}) collective-permute-start(bf16[1024,1024]{1,0:T(8,128)(2,1)} %get-tuple-element.311), channel_id=1, source_target_pairs={{0,1},{1,0},{2,3},{3,2},{4,5},{5,4},{6,7},{7,6},{8,9},{9,8},{10,11... | collective-permute-start | bytes 6291464 | tf_op jit(solution)/shard_map/ppermute | solution.py:479
  202.4 49.4 %collective-permute-start.23 = (bf16[256,1024]{1,0:T(8,128)(2,1)S(1)}, bf16[256,1024]{1,0:T(8,128)(2,1)S(1)}, u32[]{:S(2)}, u32[]{:S(2)}) collective-permute-start(bf16[256,1024]{1,0:T(8,128)(2,1)S(1)} %copy-done.18), channel_id=1, source_target_pairs={{0,2},{1,3},{2,0},{3,1},{4,6},{5,7},{6,4},{7,5},{8,10},{9,11},{10,... | collective-permute-start | bytes 1572872 | tf_op jit(solution)/shard_map/ppermute | solution.py:482
  204.0 58.1 %collective-permute-start.19 = (bf16[256,1024]{1,0:T(8,128)(2,1)}, bf16[256,1024]{1,0:T(8,128)(2,1)S(1)}, u32[]{:S(2)}, u32[]{:S(2)}) collective-permute-start(bf16[256,1024]{1,0:T(8,128)(2,1)} %get-tuple-element.196.refs_2_), channel_id=1, source_target_pairs={{0,2},{1,3},{2,0},{3,1},{4,6},{5,7},{6,4},{7,5},{8,10},{9,11},{10,... | collective-permute-start | bytes 1572872 | tf_op jit(solution)/shard_map/ppermute | solution.py:482
  214.4 9.7 %collective-permute-start.50 = (bf16[128,512]{1,0:T(8,128)(2,1)S(1)}, bf16[128,512]{1,0:T(8,128)(2,1)S(1)}, u32[]{:S(2)}, u32[]{:S(2)}) collective-permute-start(bf16[128,512]{1,0:T(8,128)(2,1)S(1)} %slice.578), channel_id=1, source_target_pairs={{0,8},{8,16},{16,24},{24,28},{28,20},{20,12},{12,4},{4,0},{1,9},{9... | collective-permute-start | bytes 393224 | tf_op jit(solution)/shard_map/ppermute | solution.py:420
  250.2 23.3 %collective-permute-start.53 = (bf16[128,512]{1,0:T(8,128)(2,1)S(1)}, bf16[128,512]{1,0:T(8,128)(2,1)S(1)}, u32[]{:S(2)}, u32[]{:S(2)}) collective-permute-start(bf16[128,512]{1,0:T(8,128)(2,1)S(1)} %add_convert_fusion.39), channel_id=1, source_target_pairs={{0,8},{8,16},{16,24},{24,28},{28,20},{20,12},{12,4},{4,0},{1,9},{9... | collective-permute-start | bytes 393224 | tf_op jit(solution)/shard_map/ppermute | solution.py:420
  251.8 22.5 %collective-permute-start.67 = (bf16[128,512]{1,0:T(8,128)(2,1)S(1)}, bf16[128,512]{1,0:T(8,128)(2,1)S(1)}, u32[]{:S(2)}, u32[]{:S(2)}) collective-permute-start(bf16[128,512]{1,0:T(8,128)(2,1)S(1)} %add_convert_fusion.27), channel_id=1, source_target_pairs={{8,0},{16,8},{24,16},{28,24},{20,28},{12,20},{4,12},{0,4},{9,1},{1... | collective-permute-start | bytes 393224 | tf_op jit(solution)/shard_map/ppermute | solution.py:421
  262.1 47.0 %collective-permute-start.24 = (bf16[256,1024]{1,0:T(8,128)(2,1)}, bf16[256,1024]{1,0:T(8,128)(2,1)S(1)}, u32[]{:S(2)}, u32[]{:S(2)}) collective-permute-start(bf16[256,1024]{1,0:T(8,128)(2,1)} %get-tuple-element.223.mine), channel_id=1, source_target_pairs={{0,2},{1,3},{2,0},{3,1},{4,6},{5,7},{6,4},{7,5},{8,10},{9,11},{10,... | collective-permute-start | bytes 1572872 | tf_op jit(solution)/shard_map/ppermute | solution.py:482
  273.5 40.0 %collective-permute-start.20 = (bf16[256,1024]{1,0:T(8,128)(2,1)}, bf16[256,1024]{1,0:T(8,128)(2,1)S(1)}, u32[]{:S(2)}, u32[]{:S(2)}) collective-permute-start(bf16[256,1024]{1,0:T(8,128)(2,1)} %get-tuple-element.202.mine), channel_id=1, source_target_pairs={{0,2},{1,3},{2,0},{3,1},{4,6},{5,7},{6,4},{7,5},{8,10},{9,11},{10,... | collective-permute-start | bytes 1572872 | tf_op jit(solution)/shard_map/ppermute | solution.py:482
  274.4 7.9 %collective-permute-start.54 = (bf16[128,512]{1,0:T(8,128)(2,1)S(1)}, bf16[128,512]{1,0:T(8,128)(2,1)S(1)}, u32[]{:S(2)}, u32[]{:S(2)}) collective-permute-start(bf16[128,512]{1,0:T(8,128)(2,1)S(1)} %add_convert_fusion.38), channel_id=1, source_target_pairs={{0,8},{8,16},{16,24},{24,28},{28,20},{20,12},{12,4},{4,0},{1,9},{9... | collective-permute-start | bytes 393224 | tf_op jit(solution)/shard_map/ppermute | solution.py:420
  308.2 10.6 %collective-permute-start.35 = (bf16[1024,256]{1,0:T(8,128)(2,1)S(1)}, bf16[1024,256]{1,0:T(8,128)(2,1)S(1)}, u32[]{:S(2)}, u32[]{:S(2)}) collective-permute-start(bf16[1024,256]{1,0:T(8,128)(2,1)S(1)} %copy-done.57), channel_id=1, source_target_pairs={{0,1},{1,0},{2,3},{3,2},{4,5},{5,4},{6,7},{7,6},{8,9},{9,8},{10,11... | collective-permute-start | bytes 1572872 | tf_op jit(solution)/shard_map/ppermute | solution.py:479
  309.1 10.4 %collective-permute-start.36 = (bf16[1024,256]{1,0:T(8,128)(2,1)}, bf16[1024,256]{1,0:T(8,128)(2,1)S(1)}, u32[]{:S(2)}, u32[]{:S(2)}) collective-permute-start(bf16[1024,256]{1,0:T(8,128)(2,1)} %get-tuple-element.256), channel_id=1, source_target_pairs={{0,1},{1,0},{2,3},{3,2},{4,5},{5,4},{6,7},{7,6},{8,9},{9,8},{10,11... | collective-permute-start | bytes 1572872 | tf_op jit(solution)/shard_map/ppermute | solution.py:479
  319.5 19.9 %collective-permute-start.27 = (f32[19456]{0:T(1024)S(1)}, f32[19456]{0:T(1024)S(1)}, u32[]{:S(2)}, u32[]{:S(2)}) collective-permute-start(f32[19456]{0:T(1024)S(1)} %constant_dynamic-update-slice_fusion.11), channel_id=1, source_target_pairs={{0,1},{1,0},{2,3},{3,2},{4,5},{5,4},{6,7},{7,6},{8,9},{9,8},{10,11... | collective-permute-start | bytes 233480 | tf_op jit(solution)/shard_map/ppermute | solution.py:479
  342.5 8.9 %collective-permute-start.28 = (f32[2432]{0:T(1024)S(1)}, f32[2432]{0:T(1024)S(1)}, u32[]{:S(2)}, u32[]{:S(2)}) collective-permute-start(f32[2432]{0:T(1024)S(1)} %get-tuple-element.315), channel_id=1, source_target_pairs={{0,4},{4,8},{8,12},{12,16},{16,20},{20,24},{24,28},{28,0},{1,5},{5... | collective-permute-start | bytes 29192 | tf_op jit(solution)/shard_map/ppermute | solution.py:435
  343.0 9.5 %collective-permute-start.34 = (f32[2432]{0:T(1024)S(1)}, f32[2432]{0:T(1024)S(1)}, u32[]{:S(2)}, u32[]{:S(2)}) collective-permute-start(f32[2432]{0:T(1024)S(1)} %get-tuple-element.316), channel_id=1, source_target_pairs={{0,28},{4,0},{8,4},{12,8},{16,12},{20,16},{24,20},{28,24},{1,29},{... | collective-permute-start | bytes 29192 | tf_op jit(solution)/shard_map/ppermute | solution.py:435
  348.3 8.8 %collective-permute-start.33 = (f32[2432]{0:T(1024)S(1)}, f32[2432]{0:T(1024)S(1)}, u32[]{:S(2)}, u32[]{:S(2)}) collective-permute-start(f32[2432]{0:T(1024)S(1)} %get-tuple-element.317), channel_id=1, source_target_pairs={{0,24},{4,28},{8,0},{12,4},{16,8},{20,12},{24,16},{28,20},{1,25},{... | collective-permute-start | bytes 29192 | tf_op jit(solution)/shard_map/ppermute | solution.py:435
  348.9 8.3 %collective-permute-start.32 = (f32[2432]{0:T(1024)S(1)}, f32[2432]{0:T(1024)S(1)}, u32[]{:S(2)}, u32[]{:S(2)}) collective-permute-start(f32[2432]{0:T(1024)S(1)} %get-tuple-element.318), channel_id=1, source_target_pairs={{0,20},{4,24},{8,28},{12,0},{16,4},{20,8},{24,12},{28,16},{1,21},{... | collective-permute-start | bytes 29192 | tf_op jit(solution)/shard_map/ppermute | solution.py:435
  349.0 8.7 %collective-permute-start.31 = (f32[2432]{0:T(1024)S(1)}, f32[2432]{0:T(1024)S(1)}, u32[]{:S(2)}, u32[]{:S(2)}) collective-permute-start(f32[2432]{0:T(1024)S(1)} %get-tuple-element.319), channel_id=1, source_target_pairs={{0,16},{4,20},{8,24},{12,28},{16,0},{20,4},{24,8},{28,12},{1,17},{... | collective-permute-start | bytes 29192 | tf_op jit(solution)/shard_map/ppermute | solution.py:435
  357.1 81.3 %collective-permute-start.71 = (bf16[1024,1024]{1,0:T(8,128)(2,1)}, bf16[1024,1024]{1,0:T(8,128)(2,1)}, u32[]{:S(2)}, u32[]{:S(2)}) collective-permute-start(bf16[1024,1024]{1,0:T(8,128)(2,1)} %get-tuple-element.295), channel_id=1, source_target_pairs={{0,1},{1,0},{2,3},{3,2},{4,5},{5,4},{6,7},{7,6},{8,9},{9,8},{10,11... | collective-permute-start | bytes 6291464 | tf_op jit(solution)/shard_map/ppermute | solution.py:479
  357.2 83.2 %collective-permute-start.72 = (bf16[1024,1024]{1,0:T(8,128)(2,1)}, bf16[1024,1024]{1,0:T(8,128)(2,1)}, u32[]{:S(2)}, u32[]{:S(2)}) collective-permute-start(bf16[1024,1024]{1,0:T(8,128)(2,1)} %get-tuple-element.296), channel_id=1, source_target_pairs={{0,1},{1,0},{2,3},{3,2},{4,5},{5,4},{6,7},{7,6},{8,9},{9,8},{10,11... | collective-permute-start | bytes 6291464 | tf_op jit(solution)/shard_map/ppermute | solution.py:479
  357.7 93.8 %collective-permute-start.26 = (f32[256,1024]{1,0:T(8,128)S(1)}, f32[256,1024]{1,0:T(8,128)}, u32[]{:S(2)}, u32[]{:S(2)}) collective-permute-start(f32[256,1024]{1,0:T(8,128)S(1)} %copy-done.17), channel_id=1, source_target_pairs={{0,1},{1,0},{2,3},{3,2},{4,5},{5,4},{6,7},{7,6},{8,9},{9,8},{10,11... | collective-permute-start | bytes 3145736 | tf_op jit(solution)/shard_map/ppermute | solution.py:479
  363.7 12.6 %collective-permute-start.96 = (bf16[128,1024]{1,0:T(8,128)(2,1)S(1)}, bf16[128,1024]{1,0:T(8,128)(2,1)S(1)}, u32[]{:S(2)}, u32[]{:S(2)}) collective-permute-start(bf16[128,1024]{1,0:T(8,128)(2,1)S(1)} %slice.526), channel_id=1, source_target_pairs={{8,0},{16,8},{24,16},{28,24},{20,28},{12,20},{4,12},{0,4},{9,1},{1... | collective-permute-start | bytes 786440 | tf_op jit(solution)/shard_map/ppermute | solution.py:421
  383.8 16.2 %collective-permute-start.97 = (bf16[128,1024]{1,0:T(8,128)(2,1)S(1)}, bf16[128,1024]{1,0:T(8,128)(2,1)S(1)}, u32[]{:S(2)}, u32[]{:S(2)}) collective-permute-start(bf16[128,1024]{1,0:T(8,128)(2,1)S(1)} %add_convert_fusion.5), channel_id=1, source_target_pairs={{8,0},{16,8},{24,16},{28,24},{20,28},{12,20},{4,12},{0,4},{9,1},{1... | collective-permute-start | bytes 786440 | tf_op jit(solution)/shard_map/ppermute | solution.py:421
  413.3 40.5 %collective-permute-start.25 = (f32[256,1024]{1,0:T(8,128)}, f32[256,1024]{1,0:T(8,128)}, u32[]{:S(2)}, u32[]{:S(2)}) collective-permute-start(f32[256,1024]{1,0:T(8,128)} %get-tuple-element.203), channel_id=1, source_target_pairs={{0,1},{1,0},{2,3},{3,2},{4,5},{5,4},{6,7},{7,6},{8,9},{9,8},{10,11... | collective-permute-start | bytes 3145736 | tf_op jit(solution)/shard_map/ppermute | solution.py:479
  436.9 22.0 %collective-permute-start.99 = (bf16[128,1024]{1,0:T(8,128)(2,1)}, bf16[128,1024]{1,0:T(8,128)(2,1)S(1)}, u32[]{:S(2)}, u32[]{:S(2)}) collective-permute-start(bf16[128,1024]{1,0:T(8,128)(2,1)} %add_convert_fusion.3), channel_id=1, source_target_pairs={{8,0},{16,8},{24,16},{28,24},{20,28},{12,20},{4,12},{0,4},{9,1},{1... | collective-permute-start | bytes 786440 | tf_op jit(solution)/shard_map/ppermute | solution.py:421
  438.4 20.6 %collective-permute-start.85 = (bf16[128,1024]{1,0:T(8,128)(2,1)}, bf16[128,1024]{1,0:T(8,128)(2,1)S(1)}, u32[]{:S(2)}, u32[]{:S(2)}) collective-permute-start(bf16[128,1024]{1,0:T(8,128)(2,1)} %add_convert_fusion.15), channel_id=1, source_target_pairs={{0,8},{8,16},{16,24},{24,28},{28,20},{20,12},{12,4},{4,0},{1,9},{9... | collective-permute-start | bytes 786440 | tf_op jit(solution)/shard_map/ppermute | solution.py:420
  451.4 9.7 %collective-permute-start.89 = (bf16[128,1024]{1,0:T(8,128)(2,1)S(1)}, bf16[128,1024]{1,0:T(8,128)(2,1)S(1)}, u32[]{:S(2)}, u32[]{:S(2)}) collective-permute-start(bf16[128,1024]{1,0:T(8,128)(2,1)S(1)} %slice.518), channel_id=1, source_target_pairs={{8,0},{16,8},{24,16},{28,24},{20,28},{12,20},{4,12},{0,4},{9,1},{1... | collective-permute-start | bytes 786440 | tf_op jit(solution)/shard_map/ppermute | solution.py:421
  451.5 9.8 %collective-permute-start.73 = (bf16[128,1024]{1,0:T(8,128)(2,1)S(1)}, bf16[128,1024]{1,0:T(8,128)(2,1)S(1)}, u32[]{:S(2)}, u32[]{:S(2)}) collective-permute-start(bf16[128,1024]{1,0:T(8,128)(2,1)S(1)} %slice.500), channel_id=1, source_target_pairs={{0,8},{8,16},{16,24},{24,28},{28,20},{20,12},{12,4},{4,0},{1,9},{9... | collective-permute-start | bytes 786440 | tf_op jit(solution)/shard_map/ppermute | solution.py:420
  458.9 9.3 %collective-permute-start.100 = (bf16[128,1024]{1,0:T(8,128)(2,1)S(1)}, bf16[128,1024]{1,0:T(8,128)(2,1)S(1)}, u32[]{:S(2)}, u32[]{:S(2)}) collective-permute-start(bf16[128,1024]{1,0:T(8,128)(2,1)S(1)} %add_convert_fusion.2), channel_id=1, source_target_pairs={{8,0},{16,8},{24,16},{28,24},{20,28},{12,20},{4,12},{0,4},{9,1},{1... | collective-permute-start | bytes 786440 | tf_op jit(solution)/shard_map/ppermute | solution.py:421
  459.1 14.9 %collective-permute-start.86 = (bf16[128,1024]{1,0:T(8,128)(2,1)S(1)}, bf16[128,1024]{1,0:T(8,128)(2,1)S(1)}, u32[]{:S(2)}, u32[]{:S(2)}) collective-permute-start(bf16[128,1024]{1,0:T(8,128)(2,1)S(1)} %add_convert_fusion.14), channel_id=1, source_target_pairs={{0,8},{8,16},{16,24},{24,28},{28,20},{20,12},{12,4},{4,0},{1,9},{9... | collective-permute-start | bytes 786440 | tf_op jit(solution)/shard_map/ppermute | solution.py:420
  461.2 12.4 %collective-permute-start.90 = (bf16[128,1024]{1,0:T(8,128)(2,1)S(1)}, bf16[128,1024]{1,0:T(8,128)(2,1)S(1)}, u32[]{:S(2)}, u32[]{:S(2)}) collective-permute-start(bf16[128,1024]{1,0:T(8,128)(2,1)S(1)} %add_convert_fusion.11), channel_id=1, source_target_pairs={{8,0},{16,8},{24,16},{28,24},{20,28},{12,20},{4,12},{0,4},{9,1},{1... | collective-permute-start | bytes 786440 | tf_op jit(solution)/shard_map/ppermute | solution.py:421
  461.4 14.5 %collective-permute-start.74 = (bf16[128,1024]{1,0:T(8,128)(2,1)S(1)}, bf16[128,1024]{1,0:T(8,128)(2,1)S(1)}, u32[]{:S(2)}, u32[]{:S(2)}) collective-permute-start(bf16[128,1024]{1,0:T(8,128)(2,1)S(1)} %add_convert_fusion.23), channel_id=1, source_target_pairs={{0,8},{8,16},{16,24},{24,28},{28,20},{20,12},{12,4},{4,0},{1,9},{9... | collective-permute-start | bytes 786440 | tf_op jit(solution)/shard_map/ppermute | solution.py:420
  468.3 14.9 %collective-permute-start.101 = (bf16[128,1024]{1,0:T(8,128)(2,1)S(1)}, bf16[128,1024]{1,0:T(8,128)(2,1)S(1)}, u32[]{:S(2)}, u32[]{:S(2)}) collective-permute-start(bf16[128,1024]{1,0:T(8,128)(2,1)S(1)} %add_convert_fusion.1), channel_id=1, source_target_pairs={{8,0},{16,8},{24,16},{28,24},{20,28},{12,20},{4,12},{0,4},{9,1},{1... | collective-permute-start | bytes 786440 | tf_op jit(solution)/shard_map/ppermute | solution.py:421
  473.7 9.2 %collective-permute-start.91 = (bf16[128,1024]{1,0:T(8,128)(2,1)S(1)}, bf16[128,1024]{1,0:T(8,128)(2,1)S(1)}, u32[]{:S(2)}, u32[]{:S(2)}) collective-permute-start(bf16[128,1024]{1,0:T(8,128)(2,1)S(1)} %add_convert_fusion.10), channel_id=1, source_target_pairs={{8,0},{16,8},{24,16},{28,24},{20,28},{12,20},{4,12},{0,4},{9,1},{1... | collective-permute-start | bytes 786440 | tf_op jit(solution)/shard_map/ppermute | solution.py:421
  474.1 16.9 %collective-permute-start.87 = (bf16[128,1024]{1,0:T(8,128)(2,1)S(1)}, bf16[128,1024]{1,0:T(8,128)(2,1)S(1)}, u32[]{:S(2)}, u32[]{:S(2)}) collective-permute-start(bf16[128,1024]{1,0:T(8,128)(2,1)S(1)} %add_convert_fusion.13), channel_id=1, source_target_pairs={{0,8},{8,16},{16,24},{24,28},{28,20},{20,12},{12,4},{4,0},{1,9},{9... | collective-permute-start | bytes 786440 | tf_op jit(solution)/shard_map/ppermute | solution.py:420
  476.0 10.5 %collective-permute-start.75 = (bf16[128,1024]{1,0:T(8,128)(2,1)S(1)}, bf16[128,1024]{1,0:T(8,128)(2,1)S(1)}, u32[]{:S(2)}, u32[]{:S(2)}) collective-permute-start(bf16[128,1024]{1,0:T(8,128)(2,1)S(1)} %add_convert_fusion.22), channel_id=1, source_target_pairs={{0,8},{8,16},{16,24},{24,28},{28,20},{20,12},{12,4},{4,0},{1,9},{9... | collective-permute-start | bytes 786440 | tf_op jit(solution)/shard_map/ppermute | solution.py:420
  483.3 16.1 %collective-permute-start.102 = (bf16[128,1024]{1,0:T(8,128)(2,1)S(1)}, bf16[128,1024]{1,0:T(8,128)(2,1)S(1)}, u32[]{:S(2)}, u32[]{:S(2)}) collective-permute-start(bf16[128,1024]{1,0:T(8,128)(2,1)S(1)} %add_convert_fusion), channel_id=1, source_target_pairs={{8,0},{16,8},{24,16},{28,24},{20,28},{12,20},{4,12},{0,4},{9,1},{1... | collective-permute-start | bytes 786440 | tf_op jit(solution)/shard_map/ppermute | solution.py:421
  490.6 8.4 %collective-permute-start.93 = (bf16[128,1024]{1,0:T(8,128)(2,1)S(1)}, bf16[128,1024]{1,0:T(8,128)(2,1)S(1)}, u32[]{:S(2)}, u32[]{:S(2)}) collective-permute-start(bf16[128,1024]{1,0:T(8,128)(2,1)S(1)} %add_convert_fusion.8), channel_id=1, source_target_pairs={{8,0},{16,8},{24,16},{28,24},{20,28},{12,20},{4,12},{0,4},{9,1},{1... | collective-permute-start | bytes 786440 | tf_op jit(solution)/shard_map/ppermute | solution.py:421
  491.1 15.3 %collective-permute-start.88 = (bf16[128,1024]{1,0:T(8,128)(2,1)S(1)}, bf16[128,1024]{1,0:T(8,128)(2,1)S(1)}, u32[]{:S(2)}, u32[]{:S(2)}) collective-permute-start(bf16[128,1024]{1,0:T(8,128)(2,1)S(1)} %add_convert_fusion.12), channel_id=1, source_target_pairs={{0,8},{8,16},{16,24},{24,28},{28,20},{20,12},{12,4},{4,0},{1,9},{9... | collective-permute-start | bytes 786440 | tf_op jit(solution)/shard_map/ppermute | solution.py:420
  494.0 9.1 %collective-permute-start.77 = (bf16[128,1024]{1,0:T(8,128)(2,1)S(1)}, bf16[128,1024]{1,0:T(8,128)(2,1)S(1)}, u32[]{:S(2)}, u32[]{:S(2)}) collective-permute-start(bf16[128,1024]{1,0:T(8,128)(2,1)S(1)} %add_convert_fusion.20), channel_id=1, source_target_pairs={{0,8},{8,16},{16,24},{24,28},{28,20},{20,12},{12,4},{4,0},{1,9},{9... | collective-permute-start | bytes 786440 | tf_op jit(solution)/shard_map/ppermute | solution.py:420
  (97 other events, 586.1 us)
